TPU v7x, 32 devices: a whole 2x2x4 slice. The times are simulated.
32 devices in a mesh: section: 2 (over core), dp: 8 (over z, y), mp: 2 (over x).
Axes of the slice: x: 2, y: 2, z: 4, core: 2. Of those that a mesh axis runs over, the one named last changes fastest.
Arguments:
- block_input: bfloat16 [2, 1024, 768], P(None, ('dp', 'mp')), may hold values from -6 to 6
- out_cotangent: bfloat16 [2, 1024, 768], P(None, ('dp', 'mp')), may hold values from -6 to 6
- seq_starts: int32 [2, 8, 2], P(None, 'dp'), may hold values from 0 to 128, as said below
- seq_lengths: int32 [2, 8, 2], P(None, 'dp'), may hold values from 0 to 128, as said below
- mixer_gain: float32 [2, 768], P('section'), may hold values from 0.5 to 1.5
- qkv_weight: bfloat16 [2, 3, 768, 768], P('section', None, None, 'mp'), may hold values from -0.21875 to 0.21875
- feature_weight: bfloat16 [2, 12, 64, 64], P('section', 'mp'), may hold values from -1.5 to 1.5
- mixer_weight: bfloat16 [2, 768, 768], P('section', 'mp'), may hold values from -1.75 to 1.75
- ffn_gain: float32 [2, 768], P('section'), may hold values from 0.5 to 1.5
- up_weight: bfloat16 [2, 768, 3072], P('section', None, 'mp'), may hold values from -0.21875 to 0.21875
- down_weight: bfloat16 [2, 3072, 768], P('section', 'mp'), may hold values from -0.109375 to 0.109375
Outputs:
- activations: bfloat16 [2, 2, 1024, 768], P('section', None, ('dp', 'mp'))
- input_grads: bfloat16 [2, 2, 1024, 768], P('section', None, ('dp', 'mp'))
- mixer_gain_grad: float32 [2, 768], P('section')
- qkv_weight_grad: float32 [2, 3, 768, 768], P('section', None, None, 'mp')
- feature_weight_grad: float32 [2, 12, 64, 64], P('section', 'mp')
- mixer_weight_grad: float32 [2, 768, 768], P('section', 'mp')
- ffn_gain_grad: float32 [2, 768], P('section')
- up_weight_grad: float32 [2, 768, 3072], P('section', None, 'mp')
- down_weight_grad: float32 [2, 3072, 768], P('section', 'mp')
Inputs may be any that keep to these rules, and one draw needn't show every extreme that they name: `seq_starts`: in each buffer the offsets rise, are multiples of 64, the first is 0, and slots after the last sequence hold 128; a sequence's span runs to the next offset or to the buffer's end. In every buffer one sequence begins in the first 64 rows and ends in the last 64 rows. `seq_lengths`: A sequence's length lies within the last 64 positions of its span; in every buffer the longest sequence fills its span of 128 tokens. Unused slots, and a trailing span that holds no sequence, have length 0.
All inputs are finite; a program needn't handle non-finite values.
Results may differ from a plain program's by a relative error of at most 0.03.
Values may be sent and summed in bfloat16 or wider, within the bound.
A program may use at most 128 MiB of HBM per device.

v0:
```python
import jax
import jax.numpy as jnp
from jax import lax
from jax.sharding import PartitionSpec as P

STRETCH = 64


EXACT_PRECISION = lax.Precision.HIGHEST


def shifted(shard, axis, by):
    size = lax.axis_size(axis)
    pairs = [(i, i + by) for i in range(size) if 0 <= i + by < size]
    return lax.ppermute(shard, axis, pairs)


def layer_norm(residual, gain):
    row_mean = jnp.mean(residual, axis=-1, keepdims=True)
    centered = residual - row_mean
    row_var = jnp.mean(centered * centered, axis=-1, keepdims=True)
    return centered * lax.rsqrt(row_var + 1e-05) * gain


def hedgehog(logits):
    return jnp.concatenate(
        [jax.nn.softmax(logits, axis=-1), jax.nn.softmax(-logits, axis=-1)], axis=-1
    )


def linear_mix(q_feat, k_feat, values, same_doc):
    row_total, head_count, feat_count = q_feat.shape
    value_width = values.shape[2]
    blocks = same_doc.shape[0]
    block_size = row_total // blocks
    q_blocks = q_feat.reshape(blocks, block_size, head_count, feat_count)
    k_blocks = k_feat.reshape(blocks, block_size, head_count, feat_count)
    v_blocks = values.reshape(blocks, block_size, head_count, value_width)
    lower_mask = (jnp.arange(block_size)[:, None] >= jnp.arange(block_size)[None, :]).astype(
        jnp.float32
    )
    scores = (
        jnp.einsum(
            "cihf,cjhf->chij",
            q_blocks,
            k_blocks,
            preferred_element_type=jnp.float32,
            precision=EXACT_PRECISION,
        )
        * lower_mask
    )
    numerator = jnp.einsum(
        "chij,cjhe->cihe", scores, v_blocks.astype(jnp.float32), precision=EXACT_PRECISION
    )
    denominator = jnp.transpose(jnp.sum(scores, axis=3), (0, 2, 1))
    block_kv = jnp.einsum(
        "cjhf,cjhe->chfe",
        k_blocks,
        v_blocks,
        preferred_element_type=jnp.float32,
        precision=EXACT_PRECISION,
    )
    block_keys = jnp.sum(k_blocks.astype(jnp.float32), axis=1)
    carried = jnp.einsum("cd,dhfe->chfe", same_doc, block_kv, precision=EXACT_PRECISION)
    carried_keys = jnp.einsum("cd,dhf->chf", same_doc, block_keys, precision=EXACT_PRECISION)
    q_wide = q_blocks.astype(jnp.float32)
    numerator = numerator + jnp.einsum(
        "cihf,chfe->cihe", q_wide, carried, precision=EXACT_PRECISION
    )
    denominator = denominator + jnp.einsum(
        "cihf,chf->cih", q_wide, carried_keys, precision=EXACT_PRECISION
    )
    return (numerator / denominator[..., None]).reshape(row_total, head_count * value_width)


def doc_tables(starts, lengths, row_total, block_size, row_offset, row_count):
    blocks = row_total // block_size
    block_pos = jnp.arange(blocks, dtype=jnp.int32) * block_size
    block_doc = jnp.sum((starts[None, :] <= block_pos[:, None]).astype(jnp.int32), axis=1)
    block_order = jnp.arange(blocks, dtype=jnp.int32)
    same_doc = (
        (block_doc[:, None] == block_doc[None, :]) & (block_order[None, :] < block_order[:, None])
    ).astype(jnp.float32)
    positions = row_offset + jnp.arange(row_count, dtype=jnp.int32)
    doc_begin = jnp.max(
        jnp.where(starts[None, :] <= positions[:, None], starts[None, :], 0), axis=1
    )
    length_of = jnp.sum(
        jnp.where(starts[None, :] == doc_begin[:, None], lengths[None, :], 0), axis=1
    )
    live_rows = (positions - doc_begin < length_of).astype(jnp.float32)
    return (same_doc, live_rows)


def local_tables(starts, same_full, row_offset, local_rows):
    local_blocks = local_rows // STRETCH
    first_block = row_offset // STRETCH
    same_local = lax.dynamic_slice(
        same_full, (first_block, first_block), (local_blocks, local_blocks)
    )
    positions = row_offset + jnp.arange(local_blocks, dtype=jnp.int32) * STRETCH
    block_begin = jnp.max(
        jnp.where(starts[None, :] <= positions[:, None], starts[None, :], 0), axis=1
    )
    carry_mask = (block_begin < row_offset).astype(jnp.float32)
    block_doc = jnp.sum((starts[None, :] <= positions[:, None]).astype(jnp.int32), axis=1)
    tail_mask = (block_doc == block_doc[local_blocks - 1]).astype(jnp.float32)
    inside = ((starts >= row_offset) & (starts < row_offset + local_rows)).astype(jnp.float32)
    keep_flag = 1.0 - jnp.max(inside)
    return (same_local, carry_mask, tail_mask, keep_flag)


def feature_parts(normalized_rows, query_key_value_matrix, feature_map):
    row_total = normalized_rows.shape[0]
    head_count = feature_map.shape[0]
    head_size = feature_map.shape[1]
    projected_rows = jnp.einsum(
        "my,qyt->qmt", normalized_rows, query_key_value_matrix, preferred_element_type=jnp.float32
    ).astype(jnp.bfloat16)
    by_head = projected_rows.reshape(3, row_total, head_count, head_size)
    q_logit = jnp.einsum(
        "nhd,hde->nhe", by_head[0], feature_map, preferred_element_type=jnp.float32
    )
    k_logit = jnp.einsum(
        "nhd,hde->nhe", by_head[1], feature_map, preferred_element_type=jnp.float32
    )
    q_feat = hedgehog(q_logit).astype(jnp.bfloat16)
    k_feat = hedgehog(k_logit).astype(jnp.bfloat16)
    return (by_head, q_logit, k_logit, q_feat, k_feat)


def forward(weights, residual, same_doc):
    (
        first_gain,
        query_key_value_matrix,
        feature_map,
        out_matrix,
        second_gain,
        up_matrix,
        down_matrix,
    ) = weights
    normalized_rows = lax.all_gather(
        layer_norm(residual, first_gain).astype(jnp.bfloat16), "mp", axis=0, tiled=True
    )
    by_head, q_logit, k_logit, q_feat, k_feat = feature_parts(
        normalized_rows, query_key_value_matrix, feature_map
    )
    mixed = linear_mix(q_feat, k_feat, by_head[2], same_doc).astype(jnp.bfloat16)
    resid_mid = residual + lax.psum_scatter(
        jnp.dot(mixed, out_matrix, preferred_element_type=jnp.float32).astype(jnp.bfloat16),
        "mp",
        scatter_dimension=0,
        tiled=True,
    ).astype(jnp.float32)
    normed_mid = lax.all_gather(
        layer_norm(resid_mid, second_gain).astype(jnp.bfloat16), "mp", axis=0, tiled=True
    )
    hidden = jax.nn.gelu(jnp.dot(normed_mid, up_matrix, preferred_element_type=jnp.float32)).astype(
        jnp.bfloat16
    )
    result = resid_mid + lax.psum_scatter(
        jnp.dot(hidden, down_matrix, preferred_element_type=jnp.float32).astype(jnp.bfloat16),
        "mp",
        scatter_dimension=0,
        tiled=True,
    ).astype(jnp.float32)
    return (result, normalized_rows, normed_mid, resid_mid)


def feature_back(
    normalized_rows, feature_map, by_head, q_logit, k_logit, grad_qf, grad_kf, grad_values
):
    row_total = normalized_rows.shape[0]
    _, q_feat_back = jax.vjp(hedgehog, q_logit)
    _, k_feat_back = jax.vjp(hedgehog, k_logit)
    grad_ql = q_feat_back(grad_qf)[0].astype(jnp.bfloat16)
    grad_kl = k_feat_back(grad_kf)[0].astype(jnp.bfloat16)
    feature_grad = jnp.einsum(
        "nhd,nhe->hde", by_head[0], grad_ql, preferred_element_type=jnp.float32
    )
    feature_grad = feature_grad + jnp.einsum(
        "nhd,nhe->hde", by_head[1], grad_kl, preferred_element_type=jnp.float32
    )
    grad_query = jnp.einsum(
        "nhe,hde->nhd", grad_ql, feature_map, preferred_element_type=jnp.float32
    ).astype(jnp.bfloat16)
    grad_keys = jnp.einsum(
        "nhe,hde->nhd", grad_kl, feature_map, preferred_element_type=jnp.float32
    ).astype(jnp.bfloat16)
    projection_gradient = jnp.stack(
        [grad_query, grad_keys, grad_values.astype(jnp.bfloat16)]
    ).reshape(3, row_total, -1)
    query_key_value_gradient = jnp.einsum(
        "cr,tcl->trl", normalized_rows, projection_gradient, preferred_element_type=jnp.float32
    )
    return (feature_grad, projection_gradient, query_key_value_gradient)


def ffn_back_local(weights, normed_mid, grad_down):
    up_matrix, down_matrix = (weights[5], weights[6])
    pre_act = jnp.dot(normed_mid, up_matrix, preferred_element_type=jnp.float32)
    hidden, gelu_back = jax.vjp(jax.nn.gelu, pre_act)
    hidden = hidden.astype(jnp.bfloat16)
    grad_hidden = jnp.einsum(
        "nd,fd->nf", grad_down, down_matrix, preferred_element_type=jnp.float32
    )
    down_grad = jnp.einsum("nf,nd->fd", hidden, grad_down, preferred_element_type=jnp.float32)
    grad_pre = gelu_back(grad_hidden)[0].astype(jnp.bfloat16)
    up_grad = jnp.einsum("nd,nf->df", normed_mid, grad_pre, preferred_element_type=jnp.float32)
    return (grad_pre, up_grad, down_grad)


def backward(weights, kept, same_doc, grad_out):
    (
        first_gain,
        query_key_value_matrix,
        feature_map,
        out_matrix,
        second_gain,
        up_matrix,
        down_matrix,
    ) = weights
    residual, normalized_rows, normed_mid, resid_mid = kept
    grad_down = lax.all_gather(grad_out.astype(jnp.bfloat16), "mp", axis=0, tiled=True)
    grad_pre, up_grad, down_grad = ffn_back_local(weights, normed_mid, grad_down)
    grad_normed_mid = lax.psum_scatter(
        jnp.einsum("nf,df->nd", grad_pre, up_matrix, preferred_element_type=jnp.float32).astype(
            jnp.bfloat16
        ),
        "mp",
        scatter_dimension=0,
        tiled=True,
    ).astype(jnp.float32)
    _, second_norm_back = jax.vjp(layer_norm, resid_mid, second_gain)
    grad_mid_norm, second_gain_grad = second_norm_back(grad_normed_mid)
    grad_mid = grad_out + grad_mid_norm
    grad_branch = lax.all_gather(grad_mid.astype(jnp.bfloat16), "mp", axis=0, tiled=True)
    by_head, q_logit, k_logit, q_feat, k_feat = feature_parts(
        normalized_rows, query_key_value_matrix, feature_map
    )

    def mix_local(q_part, k_part, v_part):
        return linear_mix(q_part, k_part, v_part, same_doc)

    mixed_wide, mix_back = jax.vjp(
        mix_local,
        q_feat.astype(jnp.float32),
        k_feat.astype(jnp.float32),
        by_head[2].astype(jnp.float32),
    )
    mixed = mixed_wide.astype(jnp.bfloat16)
    grad_mixed = jnp.einsum(
        "nd,ed->ne", grad_branch, out_matrix, preferred_element_type=jnp.float32
    ).astype(jnp.bfloat16)
    out_grad = jnp.einsum("ne,nd->ed", mixed, grad_branch, preferred_element_type=jnp.float32)
    grad_qf, grad_kf, grad_values = mix_back(grad_mixed.astype(jnp.float32))
    feature_grad, projection_gradient, query_key_value_gradient = feature_back(
        normalized_rows, feature_map, by_head, q_logit, k_logit, grad_qf, grad_kf, grad_values
    )
    grad_normed = lax.psum_scatter(
        jnp.einsum(
            "hpq,hgq->pg",
            projection_gradient,
            query_key_value_matrix,
            preferred_element_type=jnp.float32,
        ).astype(jnp.bfloat16),
        "mp",
        scatter_dimension=0,
        tiled=True,
    ).astype(jnp.float32)
    _, first_norm_back = jax.vjp(layer_norm, residual, first_gain)
    grad_in_norm, first_gain_grad = first_norm_back(grad_normed)
    grad_in = grad_mid + grad_in_norm
    return (
        grad_in,
        (
            first_gain_grad,
            query_key_value_gradient,
            feature_grad,
            out_grad,
            second_gain_grad,
            up_grad,
            down_grad,
        ),
    )


def fetch_slot(store, micro_slot):
    return lax.dynamic_index_in_dim(store, micro_slot, 0, keepdims=False)


def place_slot(store, value, micro_slot, active):
    return lax.dynamic_update_index_in_dim(
        store, jnp.where(active, value, fetch_slot(store, micro_slot)), micro_slot, 0
    )


def on_device(
    block_input,
    out_cotangent,
    seq_starts,
    seq_lengths,
    mixer_gain,
    qkv_weight,
    feature_weight,
    mixer_weight,
    ffn_gain,
    up_weight,
    down_weight,
):
    section_id = lax.axis_index("section")
    weights = (
        mixer_gain[0],
        qkv_weight[0],
        feature_weight[0],
        mixer_weight[0],
        ffn_gain[0],
        up_weight[0],
        down_weight[0],
    )
    micro_count, local_rows, model_width = block_input.shape
    group_rows = local_rows * lax.axis_size("mp")
    row_offset = lax.axis_index("mp") * local_rows
    same_list = []
    live_list = []
    local_list = []
    for micro_no in range(micro_count):
        starts = seq_starts[micro_no, 0]
        same_doc, live_rows = doc_tables(
            starts, seq_lengths[micro_no, 0], group_rows, STRETCH, row_offset, local_rows
        )
        same_list.append(same_doc)
        live_list.append(live_rows)
        local_list.append(local_tables(starts, same_doc, row_offset, local_rows))
    same_all = jnp.stack(same_list)
    live_all = jnp.stack(live_list)
    activations = jnp.zeros((micro_count, local_rows, model_width), jnp.bfloat16)
    kept_in = jnp.zeros((micro_count, local_rows, model_width), jnp.float32)
    kept_mid = jnp.zeros((micro_count, local_rows, model_width), jnp.float32)
    kept_normed = jnp.zeros((micro_count, group_rows, model_width), jnp.bfloat16)
    kept_normed_mid = jnp.zeros((micro_count, group_rows, model_width), jnp.bfloat16)
    held_in = jnp.zeros((local_rows, model_width), jnp.bfloat16)
    for step_no in range(micro_count + 1):
        micro_index = step_no - section_id
        active = (micro_index >= 0) & (micro_index < micro_count)
        micro_slot = jnp.clip(micro_index, 0, micro_count - 1)
        fresh_rows = block_input[min(step_no, micro_count - 1)]
        residual = jnp.where(section_id == 0, fresh_rows, held_in).astype(jnp.float32)
        result, normalized_rows, normed_mid, resid_mid = forward(
            weights, residual, fetch_slot(same_all, micro_slot)
        )
        outgoing = result.astype(jnp.bfloat16)
        activations = place_slot(activations, outgoing, micro_slot, active)
        kept_in = place_slot(kept_in, residual, micro_slot, active)
        kept_mid = place_slot(kept_mid, resid_mid, micro_slot, active)
        kept_normed = place_slot(kept_normed, normalized_rows, micro_slot, active)
        kept_normed_mid = place_slot(kept_normed_mid, normed_mid, micro_slot, active)
        if step_no < micro_count:
            held_in = shifted(outgoing, "section", 1)
    totals = tuple((jnp.zeros(weight.shape, jnp.float32) for weight in weights))
    input_grads = jnp.zeros((micro_count, local_rows, model_width), jnp.bfloat16)
    returned = jnp.zeros((local_rows, model_width), jnp.bfloat16)
    for step_no in range(micro_count + 1):
        micro_index = micro_count - step_no - section_id
        active = (micro_index >= 0) & (micro_index < micro_count)
        micro_slot = jnp.clip(micro_index, 0, micro_count - 1)
        top_grad = (
            fetch_slot(out_cotangent, micro_slot).astype(jnp.float32)
            * fetch_slot(live_all, micro_slot)[:, None]
        )
        grad_out = jnp.where(
            section_id == 1, top_grad, returned.astype(jnp.float32)
        ) * active.astype(jnp.float32)
        kept = (
            fetch_slot(kept_in, micro_slot),
            fetch_slot(kept_normed, micro_slot),
            fetch_slot(kept_normed_mid, micro_slot),
            fetch_slot(kept_mid, micro_slot),
        )
        grad_in, parts = backward(weights, kept, fetch_slot(same_all, micro_slot), grad_out)
        back_sent = grad_in.astype(jnp.bfloat16)
        input_grads = place_slot(input_grads, back_sent, micro_slot, active)
        totals = tuple((held + piece for held, piece in zip(totals, parts)))
        if step_no < micro_count:
            returned = shifted(back_sent, "section", -1)
    summed_all = lax.psum(
        (totals[0], totals[1], totals[2], totals[3], totals[4], totals[5], totals[6]), "dp"
    )
    gain_first, gain_second = lax.psum((summed_all[0], summed_all[4]), "mp")
    return (
        activations[None],
        input_grads[None],
        gain_first[None],
        summed_all[1][None],
        summed_all[2][None],
        summed_all[3][None],
        gain_second[None],
        summed_all[5][None],
        summed_all[6][None],
    )


def solution(mesh):
    in_specs = (
        P(None, ("dp", "mp"), None),
        P(None, ("dp", "mp"), None),
        P(None, "dp", None),
        P(None, "dp", None),
        P("section", None),
        P("section", None, None, "mp"),
        P("section", "mp", None, None),
        P("section", "mp", None),
        P("section", None),
        P("section", None, "mp"),
        P("section", "mp", None),
    )
    out_specs = (
        P("section", None, ("dp", "mp"), None),
        P("section", None, ("dp", "mp"), None),
        P("section", None),
        P("section", None, None, "mp"),
        P("section", "mp", None, None),
        P("section", "mp", None),
        P("section", None),
        P("section", None, "mp"),
        P("section", "mp", None),
    )
    return jax.shard_map(
        on_device, mesh=mesh, in_specs=in_specs, out_specs=out_specs, check_vma=False
    )
```

profile of v0, /device:TPU:1, one launch (start us, length us, event | category | flops | bytes accessed | tf_op | source)
XLA Modules:
  0.0 1190.8 jit_solution(13065503553559361521)
XLA Ops:
  11.3 5.2 all_gather.36
  43.1 4.3 all_gather.42
  47.4 6.7 reduce-scatter.13.cloned.1.call-done
  57.2 4.1 all_gather.37
  61.3 3.4 fusion.190
  66.4 10.6 reduce-scatter.15.cloned.1.call-done
  82.8 5.0 all_gather.38
  106.6 2.2 fusion.770
  128.2 7.6 reduce-scatter.17.cloned.1.call-done
  138.9 4.3 all_gather.39
  143.1 3.5 fusion.193
  150.1 8.8 reduce-scatter.19.cloned.1.call-done
  165.4 5.3 all_gather.40
  194.0 2.4 fusion.804
  196.5 2.4 fusion.807
  203.3 2.4 fusion.785
  205.7 2.4 fusion.788
  209.7 2.4 fusion.791
  212.1 2.4 fusion.794
  218.9 2.4 fusion.772
  221.3 2.4 fusion.775
  225.4 2.4 fusion.778
  227.8 2.4 fusion.781
  246.6 2.9 fusion.771
  346.2 2.3 fusion.784
  367.2 2.2 fusion.558
  386.0 4.1 all_gather.41
  397.7 12.2 %reduce-scatter.25.cloned.1.call-done = bf16[64,768]{1,0:T(8,128)(2,1)} async-done(((bf16[128,768]{1,0:T(8,128)(2,1)}), bf16[64,768]{1,0:T(8,128)(2,1)}) %reduce-scatter.25.cloned.1.call-update) | async-done | bytes 98320 | tf_op jit(solution)/shard_map/reduce_scatter | solution.py:226
  414.4 4.4 all_gather.43
  462.9 3.0 fusion.178
  466.5 2.2 fusion.546
  468.7 9.4 reduce-scatter.27.cloned.1.call-done
  483.0 2.6 collective-permute-start.2
  487.2 5.2 all_gather.44
  495.9 11.0 reduce-scatter.29.cloned.1.call-done
  511.4 4.5 all_gather.45
  563.1 3.0 fusion.175
  566.1 4.2 fusion.340
  571.0 7.3 reduce-scatter.31.cloned.1.call-done
  583.2 2.5 collective-permute-start.3
  587.9 5.2 all_gather.46
  596.8 4.1 fusion.484
  600.9 3.5 fusion.196
  606.2 3.6 fusion.481
  614.3 2.3 fusion.877
  616.6 4.0 fusion.341
  620.7 3.0 fusion.478
  624.6 2.4 fusion.475
  631.7 2.9 convolution_add_fusion.1
  634.6 7.3 add_bitcast_fusion
  642.0 3.0 add_bitcast_fusion.1
  649.5 4.4 all_gather.47
  659.8 2.7 fusion.342
  679.6 2.2 fusion.758
  698.7 2.9 fusion.172
  701.8 2.8 fusion.84
  705.5 5.5 add_bitcast_fusion.2
  717.9 18.3 %all-reduce = (f32[768]{0:T(1024)S(1)}, f32[768]{0:T(1024)S(1)}) all-reduce(f32[768]{0:T(1024)S(1)} %add_add_fusion.9, f32[768]{0:T(1024)S(1)} %add_add_fusion.8), channel_id=1, replica_groups=mesh['section'=2,'dp'=8,'mp'=2] {'dp'}, use_global_device_ids=true, to_apply=%region_132.133 | all-reduce | flops 1536 | bytes 12288 | tf_op jit(solution)/shard_map/psum | solution.py:386
  736.2 4.8 all-reduce.2
  742.3 426.3 %all-reduce.5.cloned.1.call-done = (f32[1,3,768,384]{2,3,1,0:T(8,128)}, f32[1,6,64,64]{3,2,1,0:T(8,128)}, f32[1,384,768]{2,1,0:T(8,128)}, f32[1,768,1536]{2,1,0:T(8,128)}, f32[1,1536,768]{2,1,0:T(8,128)}) async-done(((f32[1,3,768,384]{2,3,1,0:T(8,128)}, f32[1,6,64,64]{3,2,1,0:T(8,128)}, f32[1,384,768]{2,1,0:T(8,128)}, f32[1,768,1536]{2,1,0:T(8,128)}, f32[1,1536,768]{2,1,0:T(8,128)}), ...) | async-done | bytes 14254096 | tf_op jit(solution)/shard_map/psum | solution.py:386
  1168.6 5.2 copy.861
  1174.5 2.5 copy.1120
  1177.0 4.9 copy.1121
  1181.9 2.2 copy.1122
  (898 shorter events, 469.3 us)
Async XLA Ops:
  7.2 54.1 %copy-start = (bf16[1,768,1536]{2,1,0:T(8,128)(2,1)S(1)}, bf16[1,768,1536]{2,1,0:T(8,128)(2,1)}, u32[]{:S(2)}) copy-start(bf16[1,768,1536]{2,1,0:T(8,128)(2,1)} %param.20) | copy-start | bytes 7077892
  7.2 12.1 %copy-start.3 = (bf16[1,6,64,64]{3,2,1,0:T(8,128)(2,1)S(1)}, bf16[1,6,64,64]{3,2,1,0:T(8,128)(2,1)}, u32[]{:S(2)}) copy-start(bf16[1,6,64,64]{3,2,1,0:T(8,128)(2,1)} %param.17) | copy-start | bytes 147460
  7.2 46.8 %reduce-scatter.13.cloned.1.call-start = ((), (), s32[]{:S(2)}) async-start(), calls=%async_computation.12 | async-start | bytes 294912 | tf_op jit(solution)/shard_map/reduce_scatter | solution.py:149
  7.3 28.8 %copy-start.65 = (f32[64,64]{0,1:T(8,128)}, f32[64,64]{0,1:T(8,128)S(1)}, u32[]{:S(2)}) copy-start(f32[64,64]{0,1:T(8,128)S(1)} %fusion.543) | copy-start | bytes 49156
  22.8 13.2 %copy-start.42 = (bf16[2,64,6,64]{3,1,2,0:T(8,128)(2,1)}, bf16[2,64,6,64]{3,1,2,0:T(8,128)(2,1)S(1)}, u32[]{:S(2)}) copy-start(bf16[2,64,6,64]{3,1,2,0:T(8,128)(2,1)S(1)} %copy.682) | copy-start | bytes 294916
  33.5 72.9 %copy-start.170 = (pred[1,2,2]{2,1,0:T(4,128)(4,1)}, pred[1,2,2]{2,1,0:T(4,128)(4,1)S(1)}, u32[]{:S(2)}) copy-start(pred[1,2,2]{2,1,0:T(4,128)(4,1)S(1)} %get-tuple-element.175) | copy-start | bytes 16
  36.8 17.2 %copy-start.10 = (bf16[2,64,768]{2,1,0:T(8,128)(2,1)S(1)}, bf16[2,64,768]{2,1,0:T(8,128)(2,1)}, u32[]{:S(2)}) copy-start(bf16[2,64,768]{2,1,0:T(8,128)(2,1)} %param.11) | copy-start | bytes 589828
  40.7 36.3 %reduce-scatter.15.cloned.1.call-start = ((), (), s32[]{:S(2)}) async-start(), calls=%async_computation.13 | async-start | bytes 294912 | tf_op jit(solution)/shard_map/reduce_scatter | solution.py:161
  43.0 21.7 %copy-start.157 = (f32[64]{0:T(128)}, f32[64]{0:T(128)S(1)}, u32[]{:S(2)}) copy-start(f32[64]{0:T(128)S(1)} %get-tuple-element.170) | copy-start | bytes 772
  61.3 15.7 %copy-start.35 = (bf16[64,768]{1,0:T(8,128)(2,1)S(1)}, bf16[64,768]{1,0:T(8,128)(2,1)}, u32[]{:S(2)}) copy-start(bf16[64,768]{1,0:T(8,128)(2,1)} %reduce-scatter.13.cloned.1.call-done) | copy-start | bytes 294916
  64.8 71.0 %reduce-scatter.17.cloned.1.call-start = ((), (), s32[]{:S(2)}) async-start(), calls=%async_computation.14 | async-start | bytes 294912 | tf_op jit(solution)/shard_map/reduce_scatter | solution.py:149
  64.9 13.2 %copy-start.7 = (bf16[2,128,768]{2,1,0:T(8,128)(2,1)}, bf16[2,128,768]{2,1,0:T(8,128)(2,1)S(1)}, u32[]{:S(2)}) copy-start(bf16[2,128,768]{2,1,0:T(8,128)(2,1)S(1)} %bitcast_dynamic-update-slice_fusion.2) | copy-start | bytes 1179652
  78.2 3.2 collective-permute-start
  124.2 34.6 %reduce-scatter.19.cloned.1.call-start = ((), (), s32[]{:S(2)}) async-start(), calls=%async_computation.15 | async-start | bytes 294912 | tf_op jit(solution)/shard_map/reduce_scatter | solution.py:161
  143.1 15.7 %copy-start.34 = (bf16[64,768]{1,0:T(8,128)(2,1)S(1)}, bf16[64,768]{1,0:T(8,128)(2,1)}, u32[]{:S(2)}) copy-start(bf16[64,768]{1,0:T(8,128)(2,1)} %reduce-scatter.17.cloned.1.call-done) | copy-start | bytes 294916
  143.1 15.7 %copy-start.109 = (bf16[1,64,768]{2,1,0:T(8,128)(2,1)S(1)}, bf16[1,64,768]{2,1,0:T(8,128)(2,1)}, u32[]{:S(2)}) copy-start(bf16[1,64,768]{2,1,0:T(8,128)(2,1)} %constant_dynamic-slice_fusion.16) | copy-start | bytes 294916
  146.6 234.4 %reduce-scatter.21.cloned.1.call-start = ((), (), s32[]{:S(2)}) async-start(), calls=%async_computation.16 | async-start | bytes 294912 | tf_op jit(solution)/shard_map/reduce_scatter | solution.py:149
  150.1 12.5 %copy-start.4 = (bf16[2,128,768]{2,1,0:T(8,128)(2,1)}, bf16[2,128,768]{2,1,0:T(8,128)(2,1)S(1)}, u32[]{:S(2)}) copy-start(bf16[2,128,768]{2,1,0:T(8,128)(2,1)S(1)} %bitcast_dynamic-update-slice_fusion.7) | copy-start | bytes 1179652
  158.9 11.9 copy-start.2
  160.6 3.2 collective-permute-start.1
  367.2 42.7 %reduce-scatter.25.cloned.1.call-start = ((), (), s32[]{:S(2)}) async-start(), calls=%async_computation.18 | async-start | bytes 294912 | tf_op jit(solution)/shard_map/reduce_scatter | solution.py:226
  367.2 11.7 copy-start.71
  375.0 103.1 %copy-start.181 = (f32[64]{0:T(128)}, f32[64]{0:T(128)S(1)}, u32[]{:S(2)}) copy-start(f32[64]{0:T(128)S(1)} %broadcast_multiply_fusion.4) | copy-start | bytes 772
  395.8 17.6 %copy-start.158 = (f32[64]{0:T(128)S(1)}, f32[64]{0:T(128)}, u32[]{:S(2)}) copy-start(f32[64]{0:T(128)} %copy-done.157) | copy-start | bytes 772
  397.4 27.9 %copy-start.165 = (f32[2,64,6]{1,2,0:T(8,128)S(1)}, f32[2,64,6]{1,2,0:T(8,128)}, u32[]{:S(2)}) copy-start(f32[2,64,6]{1,2,0:T(8,128)} %get-tuple-element.114) | copy-start | bytes 9220
  397.4 80.7 %reduce-scatter.27.cloned.1.call-start = ((), (), s32[]{:S(2)}) async-start(), calls=%async_computation.19 | async-start | bytes 294912 | tf_op jit(solution)/shard_map/reduce_scatter | solution.py:260
  397.4 29.9 %copy-start.182 = (f32[64]{0:T(128)}, f32[64]{0:T(128)S(1)}, u32[]{:S(2)}) copy-start(f32[64]{0:T(128)S(1)} %broadcast_multiply_fusion.3) | copy-start | bytes 772
  412.7 16.0 %copy-start.188 = (f32[64]{0:T(128)}, f32[64]{0:T(128)S(1)}, u32[]{:S(2)}) copy-start(f32[64]{0:T(128)S(1)} %negate_multiply_fusion.5) | copy-start | bytes 772
  437.7 11.5 copy-start.134
  437.7 11.5 copy-start.135
  462.1 18.8 %copy-start.189 = (f32[64]{0:T(128)S(1)}, f32[64]{0:T(128)}, u32[]{:S(2)}) copy-start(f32[64]{0:T(128)} %copy-done.188) | copy-start | bytes 772
  465.8 41.1 %reduce-scatter.29.cloned.1.call-start = ((), (), s32[]{:S(2)}) async-start(), calls=%async_computation.20 | async-start | bytes 294912 | tf_op jit(solution)/shard_map/reduce_scatter | solution.py:226
  481.0 11.4 copy-start.197
  483.0 4.0 collective-permute-start.2
  494.2 12.7 %copy-start.183 = (f32[64]{0:T(128)S(1)}, f32[64]{0:T(128)}, u32[]{:S(2)}) copy-start(f32[64]{0:T(128)} %copy-done.182) | copy-start | bytes 772
  495.8 26.8 %copy-start.163 = (f32[2,64,6]{1,2,0:T(8,128)S(1)}, f32[2,64,6]{1,2,0:T(8,128)}, u32[]{:S(2)}) copy-start(f32[2,64,6]{1,2,0:T(8,128)} %get-tuple-element.102) | copy-start | bytes 9220
  495.8 82.5 %reduce-scatter.31.cloned.1.call-start = ((), (), s32[]{:S(2)}) async-start(), calls=%async_computation.21 | async-start | bytes 294912 | tf_op jit(solution)/shard_map/reduce_scatter | solution.py:260
  495.9 26.6 %copy-start.178 = (f32[64]{0:T(128)}, f32[64]{0:T(128)S(1)}, u32[]{:S(2)}) copy-start(f32[64]{0:T(128)S(1)} %broadcast_multiply_fusion.1) | copy-start | bytes 772
  509.7 12.8 %copy-start.186 = (f32[64]{0:T(128)}, f32[64]{0:T(128)S(1)}, u32[]{:S(2)}) copy-start(f32[64]{0:T(128)S(1)} %negate_multiply_fusion.3) | copy-start | bytes 772
  534.9 11.5 copy-start.130
  534.9 11.5 copy-start.131
  543.5 11.2 copy-start.141
  546.4 12.3 %copy-start.128 = (f32[128,6]{0,1:T(8,128)S(1)}, f32[128,6]{0,1:T(8,128)}, u32[]{:S(2)}) copy-start(f32[128,6]{0,1:T(8,128)} %get-tuple-element.200) | copy-start | bytes 9220
  546.4 12.3 %copy-start.129 = (f32[128,6]{0,1:T(8,128)S(1)}, f32[128,6]{0,1:T(8,128)}, u32[]{:S(2)}) copy-start(f32[128,6]{0,1:T(8,128)} %get-tuple-element.202) | copy-start | bytes 9220
  566.1 12.3 %copy-start.180 = (f32[64]{0:T(128)S(1)}, f32[64]{0:T(128)}, u32[]{:S(2)}) copy-start(f32[64]{0:T(128)} %broadcast_multiply_fusion.2) | copy-start | bytes 772
  566.1 15.1 %copy-start.187 = (f32[64]{0:T(128)S(1)}, f32[64]{0:T(128)}, u32[]{:S(2)}) copy-start(f32[64]{0:T(128)} %copy-done.186) | copy-start | bytes 772
  566.1 78.9 %reduce-scatter.33.cloned.1.call-start = ((), (), s32[]{:S(2)}) async-start(), calls=%async_computation.22 | async-start | bytes 294912 | tf_op jit(solution)/shard_map/reduce_scatter | solution.py:226
  581.2 12.0 %copy-start.198 = (bf16[1,1536,768]{2,1,0:T(8,128)(2,1)S(1)}, bf16[1,1536,768]{2,1,0:T(8,128)(2,1)}, u32[]{:S(2)}) copy-start(bf16[1,1536,768]{2,1,0:T(8,128)(2,1)} %param.21) | copy-start | bytes 7077892
  583.2 4.0 collective-permute-start.3
  596.6 116.4 %reduce-scatter.23.cloned.1.call-start = ((), (), s32[]{:S(2)}) async-start(), calls=%async_computation.17 | async-start | bytes 294912 | tf_op jit(solution)/shard_map/reduce_scatter | solution.py:161
  604.4 111.2 %reduce-scatter.35.cloned.1.call-start = ((), (), s32[]{:S(2)}) async-start(), calls=%async_computation.23 | async-start | bytes 294912 | tf_op jit(solution)/shard_map/reduce_scatter | solution.py:260
  645.0 14.8 %copy-start.161 = (f32[2,64,6]{1,2,0:T(8,128)S(1)}, f32[2,64,6]{1,2,0:T(8,128)}, u32[]{:S(2)}) copy-start(f32[2,64,6]{1,2,0:T(8,128)} %get-tuple-element.94) | copy-start | bytes 9220
  647.7 14.8 %copy-start.184 = (f32[64]{0:T(128)}, f32[64]{0:T(128)S(1)}, u32[]{:S(2)}) copy-start(f32[64]{0:T(128)S(1)} %negate_multiply_fusion.1) | copy-start | bytes 772
  648.4 14.1 %copy-start.55 = (bf16[2,64,6,128]{3,1,2,0:T(8,128)(2,1)S(1)}, bf16[2,64,6,128]{3,1,2,0:T(8,128)(2,1)}, u32[]{:S(2)}) copy-start(bf16[2,64,6,128]{3,1,2,0:T(8,128)(2,1)} %copy-done.54) | copy-start | bytes 589828
  675.2 11.3 copy-start.140
  676.0 11.6 copy-start.126
  676.0 11.6 copy-start.127
  701.7 466.9 %all-reduce.5.cloned.1.call-start = ((), (), s32[]{:S(2)}) async-start(), calls=%async_computation.24 | async-start | bytes 28704768 | tf_op jit(solution)/shard_map/psum | solution.py:386
  711.1 30.0 %copy-start.20 = (bf16[2,64,768]{2,1,0:T(8,128)(2,1)S(1)}, bf16[2,64,768]{2,1,0:T(8,128)(2,1)}, u32[]{:S(2)}) copy-start(bf16[2,64,768]{2,1,0:T(8,128)(2,1)} %param.12) | copy-start | bytes 589828
  711.1 29.9 %copy-start.48 = (f32[64,768]{1,0:T(8,128)S(1)}, f32[64,768]{1,0:T(8,128)}, u32[]{:S(2)}) copy-start(f32[64,768]{1,0:T(8,128)} %copy-done.47) | copy-start | bytes 589828
  711.1 29.9 %copy-start.89 = (bf16[64,768]{1,0:T(8,128)(2,1)S(1)}, bf16[64,768]{1,0:T(8,128)(2,1)}, u32[]{:S(2)}) copy-start(bf16[64,768]{1,0:T(8,128)(2,1)} %copy-done.87) | copy-start | bytes 294916
  711.1 29.9 %copy-start.155 = (f32[64]{0:T(128)S(1)}, f32[64]{0:T(128)}, u32[]{:S(2)}) copy-start(f32[64]{0:T(128)} %get-tuple-element.168) | copy-start | bytes 772
  711.2 29.9 %copy-start.185 = (f32[64]{0:T(128)S(1)}, f32[64]{0:T(128)}, u32[]{:S(2)}) copy-start(f32[64]{0:T(128)} %copy-done.184) | copy-start | bytes 772
  742.2 431.5 %copy-start.124 = (bf16[1,2,64,768]{3,2,1,0:T(8,128)(2,1)}, bf16[1,2,64,768]{3,2,1,0:T(8,128)(2,1)S(1)}, u32[]{:S(2)}) copy-start(bf16[1,2,64,768]{3,2,1,0:T(8,128)(2,1)S(1)} %fusion.524) | copy-start | bytes 589828
  (158 other events, 797.7 us)
Sparse Core Ops, SparseCore 0:
  40.8 13.1 reduce-scatter.12
  64.9 12.0 reduce-scatter.14
  124.3 11.3 reduce-scatter.16
  146.7 12.0 reduce-scatter.18
  367.3 11.1 reduce-scatter.20
  397.5 12.2 reduce-scatter.24
  466.0 12.0 reduce-scatter.26
  495.9 10.9 reduce-scatter.28
  566.2 12.0 reduce-scatter.30
  596.7 10.9 reduce-scatter.32
  609.9 10.9 reduce-scatter.22
  701.8 12.0 reduce-scatter.34
  720.2 448.3 all-reduce.4
where the time goes:
time: 1210 us; the launch traced here: 1190 us
  waiting for transfers between devices  503 us (42%)
  matrix products  234 us (19%)
  local copies, waits for them, and re-layouts  225 us (19%)
  other arithmetic  123 us (10%)
  blocking collectives  79.2 us (7%)
  between operations  17.2 us (1%)
    psum x1, waiting for transfers between devices, on_device(): lax.psum((totals[0], totals[1], totals[2], totals[3], totals[4], totals[5...  426 us
    concatenate x48, local copies, waits for them, and re-layouts, hedgehog(): jnp.concatenate([jax.nn.softmax(logits, axis=-1), jax.nn.softmax(-logits,...  70 us
    unnamed x429, local copies, waits for them, and re-layouts  50.4 us
  transfers between devices with their start and end apart: 17, of which 11 were waited for; matrix products, arithmetic and copies ran while one was open for 13% of the time, Pallas kernels for 0%

commit v1 on v0

v1 whole, which is shorter than its diff:
```python
import functools

import jax
import jax.numpy as jnp
from jax import lax
from jax.experimental import pallas as pl
from jax.experimental.pallas import tpu as pltpu
from jax.sharding import PartitionSpec as P

STRETCH = 64
GROUP = 8
LINE = 4
MESH = pl.DeviceIdType.MESH
BF = jnp.bfloat16
F32 = jnp.float32
ANY = pl.BlockSpec(memory_space=pl.ANY)
VM = pl.BlockSpec(memory_space=pltpu.VMEM)
SM = pl.BlockSpec(memory_space=pltpu.SMEM)


def dot(a, b, ca=1, cb=0):
    return lax.dot_general(a, b, (((ca,), (cb,)), ((), ())), preferred_element_type=F32)


def normed(v):
    mean = jnp.mean(v, axis=1, keepdims=True)
    c = v - mean
    rstd = lax.rsqrt(jnp.mean(c * c, axis=1, keepdims=True) + 1e-05)
    return c * rstd, rstd


def norm_back(grad, gain, xhat, rstd):
    t = grad * gain
    mean_t = jnp.mean(t, axis=1, keepdims=True)
    mean_tx = jnp.mean(t * xhat, axis=1, keepdims=True)
    return rstd * (t - mean_t - xhat * mean_tx)


def gelu_both(x):
    k = 0.7978845608028654
    x2 = x * x
    t = jnp.tanh(x * (k + (k * 0.044715) * x2))
    half = 0.5 * (1.0 + t)
    slope = half + 0.5 * x * (1.0 - t * t) * (k + (3.0 * k * 0.044715) * x2)
    return x * half, slope


def both_softmax(logit):
    up = jnp.exp(logit - jnp.max(logit, axis=0, keepdims=True))
    down = jnp.exp(jnp.min(logit, axis=0, keepdims=True) - logit)
    up = up * (1.0 / jnp.sum(up, axis=0, keepdims=True))
    down = down * (1.0 / jnp.sum(down, axis=0, keepdims=True))
    return jnp.concatenate([up.astype(BF), down.astype(BF)], axis=0)


def softmax_back(grad, feat):
    n = grad.shape[0] // 2
    g = grad * feat.astype(F32)
    p = feat.astype(F32)
    one = g[:n] - p[:n] * jnp.sum(g[:n], axis=0, keepdims=True)
    two = g[n:] - p[n:] * jnp.sum(g[n:], axis=0, keepdims=True)
    return one - two


def kernel(
    x_in, cot, starts, lengths, gain1, wqkv_h, fmap, wmix_h, gain2, up_h, down_h,
    act_o, ig_o, qkv_o, mix_o, small_o, up_o, down_o,
    wqkv, wmix, wup, wdown, rin, gin, mask,
    nrm, nrm_t, pt, vnat, qf, kf, st, mt, mtb, den_s, rmid, nm_all, gd_all, gp, rout, act, igv,
    pk3, gmid, gbr, gqk, gpt, pk4, gacc, sbuf, rbuf, pay, ybuf, zbuf, fin, ups, downs, acc_u, acc_d,
    lsem, xs, xr, cs, cr, gs, gr, ars, arr, osem,
):
    s = lax.axis_index("section")
    d = lax.axis_index("dp")
    xi = lax.axis_index("mp")
    micro, half, width = x_in.shape
    rows = 2 * half
    heads, hs = fmap.shape[1], fmap.shape[2]
    hw = heads * hs
    ff = up_h.shape[2]
    g = lax.rem(d, GROUP)
    base = d - g
    pos = lax.div(g, 2)
    par = lax.rem(g, 2)
    to_x = (s, d, 1 - xi)
    to_c = (1 - s, d, xi)
    to_y = (s, base + pos * 2 + 1 - par, xi)

    def line_pos(k):
        return lax.rem(pos + k, LINE)

    def to_line(k):
        return (s, base + line_pos(k) * 2 + par, xi)

    partners = [to_x, to_c, to_y] + [to_line(k) for k in range(1, LINE)]

    def local(src, dst, i):
        return pltpu.make_async_copy(src, dst, lsem.at[i])

    def remote(src, dst, ss, rs, to):
        return pltpu.make_async_remote_copy(
            src_ref=src, dst_ref=dst, send_sem=ss, recv_sem=rs, device_id=to, device_id_type=MESH
        )

    loads = [
        local(wqkv_h.at[0], wqkv, 0),
        local(wmix_h.at[0], wmix, 1),
        local(up_h.at[0], wup, 2),
        local(down_h.at[0], wdown, 3),
    ]
    own_x = local(x_in, rin.at[:, pl.ds(0, half)], 4)
    own_c = local(cot, gin.at[:, pl.ds(0, half)], 5)

    @pl.when(s == 0)
    def _():
        own_x.start()

    @pl.when(s == 1)
    def _():
        own_c.start()

    for c in loads:
        c.start()

    barrier = pltpu.get_barrier_semaphore()
    for to in partners:
        pl.semaphore_signal(barrier, inc=1, device_id=to, device_id_type=MESH)
    pl.semaphore_wait(barrier, len(partners))

    first_x = remote(x_in, rin.at[:, pl.ds(half, half)], xs.at[0], xr.at[0], to_x)
    first_c = remote(cot, gin.at[:, pl.ds(half, half)], xs.at[0], xr.at[0], to_x)

    @pl.when(s == 0)
    def _():
        first_x.start()

    @pl.when(s == 1)
    def _():
        first_c.start()

    jj = lax.broadcasted_iota(jnp.int32, (rows, rows), 0)
    ii = lax.broadcasted_iota(jnp.int32, (rows, rows), 1)
    j_own, i_own = jj < half, ii < half
    inside = ((j_own == i_own) & (jj <= ii)).astype(F32)
    own_first = jnp.where(xi == 0, 1.0, 0.0)
    across = jnp.where(j_own & ~i_own, own_first, jnp.where(i_own & ~j_own, 1.0 - own_first, 0.0))
    slots = starts.shape[2]
    for m in range(micro):
        n0 = jnp.int32(0)
        n1 = jnp.int32(0)
        for j in range(slots):
            n0 += jnp.where(starts[m, 0, j] <= 0, 1, 0)
            n1 += jnp.where(starts[m, 0, j] <= STRETCH, 1, 0)
        same = jnp.where(n0 == n1, 1.0, 0.0)
        mask[m] = inside + across * same

    def live_of(m, part):
        block = xi if part == 0 else 1 - xi
        begin = jnp.int32(0)
        for j in range(slots):
            begin = jnp.where(starts[m, 0, j] <= block * STRETCH, jnp.maximum(begin, starts[m, 0, j]), begin)
        length = jnp.int32(0)
        for j in range(slots):
            length += jnp.where(starts[m, 0, j] == begin, lengths[m, 0, j], 0)
        row = block * STRETCH + lax.broadcasted_iota(jnp.int32, (half, width), 0)
        return (row - begin < length).astype(F32)

    def x_swap(e, m):
        i = 1 + e * micro + m
        return remote(sbuf.at[e, m], rbuf.at[e, m], xs.at[i], xr.at[i], to_x)

    def give(e, m, part):
        part = part.astype(BF)
        sbuf[e, m, pl.ds(0, half)] = part[half:]
        sbuf[e, m, pl.ds(half, half)] = part[:half]
        x_swap(e, m).start()

    def c_copy(e, m):
        i = e * micro + m
        src, dst = ((act, rin), (igv, gin))[e]
        return remote(src.at[m], dst.at[m], cs.at[i], cr.at[i], to_c)

    def mixer_forward(m):
        if m == 0:
            @pl.when(s == 0)
            def _():
                own_x.wait()
                first_x.wait_recv()

        @pl.when(s == 1)
        def _():
            c_copy(0, m).wait_recv()

        if m == 0:
            loads[0].wait()
        r = rin[m].astype(F32)
        n = (normed(r)[0] * gain1[...]).astype(BF)
        nrm[m] = n
        for q in range(3):
            p = dot(n, wqkv[q]).astype(BF)
            if q == 2:
                vnat[m] = p
            pt[m, q] = p.T
        for h in range(heads):
            hr = pl.ds(h * hs, hs)
            w = fmap[0, h]
            qfh = both_softmax(dot(w, pt[m, 0, hr], 0, 0))
            kfh = both_softmax(dot(w, pt[m, 1, hr], 0, 0))
            qf[m, h] = qfh
            kf[m, h] = kfh
            sc = dot(kfh, qfh, 0, 0) * mask[m]
            den = 1.0 / jnp.sum(sc, axis=0, keepdims=True)
            scb = sc.astype(BF)
            st[m, h] = scb
            den_s[m, h] = jnp.broadcast_to(den, (8, rows))
            mx = dot(pt[m, 2, hr], scb) * den
            mt[m, hr] = mx
            mtb[m, hr] = mx.astype(BF)
        if m == 0:
            loads[1].wait()
        part = dot(mtb[m].T, wmix[...])
        give(0, m, part)
        rmid[m] = r + part

    def ffn_forward(m):
        x_swap(0, m).wait_recv()
        r = rmid[m] + rbuf[0, m].astype(F32)
        rmid[m] = r
        n = (normed(r)[0] * gain2[...]).astype(BF)
        nm_all[g, :, pl.ds(m * rows, rows)] = n.T
        if m == 0:
            loads[2].wait()
        h, slope = gelu_both(dot(n, wup[...]))
        h = h.astype(BF)
        gp[m] = slope.astype(BF)
        if m == 0:
            loads[3].wait()
        part = dot(h, wdown[...])
        give(1, m, part)
        rout[m] = r + part

    def end_forward(m):
        x_swap(1, m).wait_recv()
        act[m] = (rout[m] + rbuf[1, m].astype(F32)).astype(BF)

        @pl.when(s == 0)
        def _():
            c_copy(0, m).start()

        pltpu.make_async_copy(act.at[m, pl.ds(0, half)], act_o.at[0, m], osem.at[m]).start()

    gathered = (nm_all, gd_all)

    def spread(kind, k):
        ref = gathered[kind].at[g]
        i = kind * 7 + k
        return remote(ref, ref, gs.at[i], gr.at[i], to_y if k == 0 else to_line(k))

    def relay(kind, k):
        slot = lax.rem(pos - k + LINE, LINE) * 2 + par
        ref = gathered[kind].at[slot]
        i = kind * 7 + LINE - 1 + k
        return remote(ref, ref, gs.at[i], gr.at[i], to_y)

    for m in range(micro):
        mixer_forward(m)
    for m in range(micro):
        ffn_forward(m)
    for k in range(LINE):
        spread(0, k).start()
    for m in range(micro):
        end_forward(m)

    def relay_all(kind):
        for k in range(1, LINE):
            spread(kind, k).wait_recv()
            relay(kind, k).start()

    @pl.when(s == 0)
    def _():
        relay_all(0)

    def ffn_back(m):
        if m == 0:
            @pl.when(s == 1)
            def _():
                own_c.wait()
                first_c.wait_recv()

        @pl.when(s == 0)
        def _():
            c_copy(1, m).wait_recv()

        for part in range(2):
            keep = jnp.where(s == 1, live_of(m, part), 1.0)
            pr = pl.ds(part * half, half)
            gd_all[g, pl.ds(m * rows + part * half, half)] = (gin[m, pr].astype(F32) * keep).astype(BF)
        gd = gd_all[g, pl.ds(m * rows, rows)]
        gpre = (dot(gd, wdown[...], 1, 1) * gp[m].astype(F32)).astype(BF)
        part = dot(gpre, wup[...], 1, 1)
        give(2, m, part)
        pk3[m] = part

    def mixer_back(m):
        x_swap(2, m).wait_recv()
        gn = pk3[m] + rbuf[2, m].astype(F32)
        xhat, rstd = normed(rmid[m])
        gacc[1, m] = jnp.broadcast_to(jnp.sum(gn * xhat, axis=0, keepdims=True), (8, width))
        gm = gd_all[g, pl.ds(m * rows, rows)].astype(F32) + norm_back(gn, gain2[...], xhat, rstd)
        gmid[m] = gm
        gb = gm.astype(BF)
        gbr[m] = gb
        gmt = dot(wmix[...], gb, 1, 1).astype(BF)
        for h in range(heads):
            hr = pl.ds(h * hs, hs)
            den = den_s[m, h, pl.ds(0, 1)]
            go = gmt[h * hs : (h + 1) * hs].astype(F32)
            gden = -jnp.sum(go * mt[m, hr], axis=0, keepdims=True) * den
            gnum = (go * den).astype(BF)
            pad = jnp.zeros_like(gnum)
            wide = jnp.concatenate([gnum, pad] if h % 2 == 0 else [pad, gnum], axis=0)
            gst = ((dot(vnat[m, :, pl.ds((h // 2) * 2 * hs, 2 * hs)], wide) + gden) * mask[m]).astype(BF)
            qfh = qf[m, h]
            kfh = kf[m, h]
            gql = softmax_back(dot(kfh, gst), qfh).astype(BF)
            gkl = softmax_back(dot(qfh, gst, 1, 1), kfh).astype(BF)
            gv = dot(gnum, st[m, h], 1, 1).astype(BF)
            gqk[0, m, hr] = gql
            gqk[1, m, hr] = gkl
            w = fmap[0, h]
            gpt[m, 0, hr] = dot(w, gql).astype(BF)
            gpt[m, 1, hr] = dot(w, gkl).astype(BF)
            gpt[m, 2, hr] = gv
        gnt = dot(wqkv[0], gpt[m, 0]) + dot(wqkv[1], gpt[m, 1]) + dot(wqkv[2], gpt[m, 2])
        part = gnt.T
        give(3, m, part)
        pk4[m] = part
        nrm_t[m] = nrm[m].T

    def end_back(m):
        x_swap(3, m).wait_recv()
        gn = pk4[m] + rbuf[3, m].astype(F32)
        xhat, rstd = normed(rin[m].astype(F32))
        gacc[0, m] = jnp.broadcast_to(jnp.sum(gn * xhat, axis=0, keepdims=True), (8, width))
        igv[m] = (gmid[m] + norm_back(gn, gain1[...], xhat, rstd)).astype(BF)

        @pl.when(s == 1)
        def _():
            c_copy(1, m).start()

        pltpu.make_async_copy(igv.at[m, pl.ds(0, half)], ig_o.at[0, m], osem.at[micro + m]).start()

    for m in range(micro):
        ffn_back(m)
    for k in range(LINE):
        spread(1, k).start()
    for m in range(micro):
        mixer_back(m)

    for q in range(3):
        tot = dot(nrm_t[0], gpt[0, q], 1, 1)
        for m in range(1, micro):
            tot += dot(nrm_t[m], gpt[m, q], 1, 1)
        pay[pl.ds(q * width, width)] = tot.astype(BF)
    tot = dot(mtb[0], gbr[0])
    for m in range(1, micro):
        tot += dot(mtb[m], gbr[m])
    tot = tot.astype(BF)
    base_row = 3 * width
    for c in range(width // hw):
        pay[pl.ds(base_row + c * hw, hw)] = tot[:, c * hw : (c + 1) * hw]
    base_row += (width // hw) * hw
    left = lax.broadcasted_iota(jnp.int32, (hs, 2 * hs), 1) < hs
    for p in range(heads // 2):
        pr = pl.ds(p * 2 * hs, 2 * hs)
        tot = jnp.zeros((2 * hs, 2 * hs), F32)
        for m in range(micro):
            tot += dot(pt[m, 0, pr], gqk[0, m, pr], 1, 1) + dot(pt[m, 1, pr], gqk[1, m, pr], 1, 1)
        pay[pl.ds(base_row, hs), pl.ds(p * 2 * hs, 2 * hs)] = jnp.where(left, tot[:hs], tot[hs:]).astype(BF)

    for m in range(micro):
        end_back(m)

    base_row += hs
    tail = pay.shape[0] - base_row
    row = lax.broadcasted_iota(jnp.int32, (tail, hw), 0)
    block = jnp.zeros((tail, hw), F32)
    for e in range(2):
        tot = gacc[e, 0, pl.ds(0, 1)]
        for m in range(1, micro):
            tot += gacc[e, m, pl.ds(0, 1)]
        for c in range(width // hw):
            block = jnp.where(row == e * (width // hw) + c, tot[:, c * hw : (c + 1) * hw], block)
    pay[pl.ds(base_row, tail)] = block.astype(BF)

    side = pay.shape[0] // 2
    chunk = side // LINE

    def mine(c):
        return pl.ds(pl.multiple_of(par * side + c * chunk, 16), chunk)

    def other(c):
        return pl.ds(pl.multiple_of((1 - par) * side + c * chunk, 16), chunk)

    def ar_pair(k):
        c = line_pos(k)
        return remote(
            pay.at[other(c)], ybuf.at[pl.ds(pl.multiple_of(c * chunk, 16), chunk)], ars.at[k], arr.at[k], to_y
        )

    def ar_line(k):
        return remote(pay.at[mine(line_pos(k))], zbuf.at[k - 1], ars.at[3 + k], arr.at[3 + k], to_line(k))

    def ar_spread(k):
        ref = fin.at[mine(pos)]
        return remote(ref, ref, ars.at[6 + k], arr.at[6 + k], to_line(k))

    def ar_back(k):
        ref = fin.at[mine(lax.rem(pos - k + LINE, LINE))]
        return remote(ref, ref, ars.at[10 + k], arr.at[10 + k], to_y)

    order = [1, 2, 3, 0]
    for k in order:
        ar_pair(k).start()

    @pl.when(s == 1)
    def _():
        relay_all(0)

    for k in order:
        ar_pair(k).wait_recv()
        c = line_pos(k)
        yr = pl.ds(pl.multiple_of(c * chunk, 16), chunk)
        pay[mine(c)] = (pay[mine(c)].astype(F32) + ybuf[yr].astype(F32)).astype(BF)
        if k > 0:
            ar_line(k).start()

    relay_all(1)
    for kind in range(2):
        spread(kind, 0).wait_recv()
        for k in range(1, LINE):
            relay(kind, k).wait_recv()


    def ffn_grads(tile, t):
        hr = pl.ds(pl.multiple_of(t * tile, tile), tile)
        wu = wup[:, hr].T
        wd = wdown[hr]
        for i in range(GROUP):
            h, slope = gelu_both(dot(wu, nm_all[i]))
            gpre = (dot(wd, gd_all[i], 1, 1) * slope).astype(BF)
            a = dot(nm_all[i], gpre, 1, 1)
            b = dot(h.astype(BF), gd_all[i])
            if i == 0:
                acc_u[...] = a
                acc_d[...] = b
            else:
                acc_u[...] += a
                acc_d[...] += b
        ups[:, hr] = acc_u[...].astype(BF)
        downs[hr] = acc_d[...].astype(BF)

    tile = 256
    steps = ff // tile

    def some(lo, hi):
        lax.fori_loop(lo, hi, lambda t, _: (ffn_grads(tile, t), 0)[1], 0)

    some(0, steps // 2)

    mrow = mine(pos)
    tot = pay[mrow].astype(F32)
    for k in range(1, LINE):
        ar_line(k).wait_recv()
        tot += zbuf[k - 1].astype(F32)
    fin[mrow] = tot.astype(BF)
    for k in range(1, LINE):
        ar_spread(k).start()
    ar_back(0).start()

    some(steps // 2, steps)
    outs = [
        pltpu.make_async_copy(ups, up_o, osem.at[2 * micro]),
        pltpu.make_async_copy(downs, down_o, osem.at[2 * micro + 1]),
    ]
    for c in outs:
        c.start()

    for k in range(1, LINE):
        ar_spread(k).wait_recv()
        ar_back(k).start()
    for k in range(LINE):
        ar_back(k).wait_recv()

    tail_out = [pltpu.make_async_copy(fin.at[pl.ds(0, 3 * width)], qkv_o, osem.at[2 * micro + 2])]
    for c in range(width // hw):
        tail_out.append(
            pltpu.make_async_copy(
                fin.at[pl.ds(3 * width + c * hw, hw)], mix_o.at[:, pl.ds(c * hw, hw)], osem.at[2 * micro + 3 + c]
            )
        )
    n_out = 2 * micro + 3 + width // hw
    small = 3 * width + (width // hw) * hw
    tail_out.append(
        pltpu.make_async_copy(fin.at[pl.ds(small, small_o.shape[0])], small_o, osem.at[n_out])
    )
    for c in tail_out:
        c.start()

    @pl.when(s == 0)
    def _():
        first_x.wait_send()
        for m in range(micro):
            c_copy(0, m).wait_send()

    @pl.when(s == 1)
    def _():
        first_c.wait_send()
        for m in range(micro):
            c_copy(1, m).wait_send()

    for e in range(4):
        for m in range(micro):
            x_swap(e, m).wait_send()
    for kind in range(2):
        for k in range(LINE):
            spread(kind, k).wait_send()
        for k in range(1, LINE):
            relay(kind, k).wait_send()
    for k in range(LINE):
        ar_pair(k).wait_send()
        ar_back(k).wait_send()
    for k in range(1, LINE):
        ar_line(k).wait_send()
        ar_spread(k).wait_send()
    for m in range(micro):
        pltpu.make_async_copy(act.at[m, pl.ds(0, half)], act_o.at[0, m], osem.at[m]).wait()
        pltpu.make_async_copy(igv.at[m, pl.ds(0, half)], ig_o.at[0, m], osem.at[micro + m]).wait()
    for c in outs + tail_out:
        c.wait()


def on_device(x, cot, starts, lengths, gain1, wqkv, fmap, wmix, gain2, wup, wdown):
    micro, half, width = x.shape
    rows = 2 * half
    heads, hs = fmap.shape[1], fmap.shape[2]
    hw = heads * hs
    ff = wup.shape[2]
    cut = width // hw
    used = 3 * width + cut * hw + hs + 2 * cut
    unit = 2 * LINE * 16
    pay_rows = -(-used // unit) * unit
    small_rows = -(-(hs + 2 * cut) // 16) * 16
    f, b = F32, BF
    vm = pltpu.VMEM
    dma = pltpu.SemaphoreType.DMA
    out = lambda shape: jax.ShapeDtypeStruct(shape, b)
    act, ig, qkv, mix, small, up, down = pl.pallas_call(
        kernel,
        out_shape=[
            out((1, micro, half, width)),
            out((1, micro, half, width)),
            out((3 * width, hw)),
            out((hw, width)),
            out((small_rows, hw)),
            out((width, ff)),
            out((ff, width)),
        ],
        in_specs=[ANY, ANY, SM, SM, VM, ANY, VM, ANY, VM, ANY, ANY],
        out_specs=[ANY] * 7,
        scratch_shapes=[
            vm((3, width, hw), b),
            vm((hw, width), b),
            vm((width, ff), b),
            vm((ff, width), b),
            vm((micro, rows, width), b),
            vm((micro, rows, width), b),
            vm((micro, rows, rows), f),
            vm((micro, rows, width), b),
            vm((micro, width, rows), b),
            vm((micro, 3, hw, rows), b),
            vm((micro, rows, hw), b),
            vm((micro, heads, 2 * hs, rows), b),
            vm((micro, heads, 2 * hs, rows), b),
            vm((micro, heads, rows, rows), b),
            vm((micro, hw, rows), f),
            vm((micro, hw, rows), b),
            vm((micro, heads, 8, rows), f),
            vm((micro, rows, width), f),
            vm((GROUP, width, micro * rows), b),
            vm((GROUP, micro * rows, width), b),
            vm((micro, rows, ff), b),
            vm((micro, rows, width), f),
            vm((micro, rows, width), b),
            vm((micro, rows, width), b),
            vm((micro, rows, width), f),
            vm((micro, rows, width), f),
            vm((micro, rows, width), b),
            vm((2, micro, hw, rows), b),
            vm((micro, 3, hw, rows), b),
            vm((micro, rows, width), f),
            vm((2, micro, 8, width), f),
            vm((4, micro, rows, width), b),
            vm((4, micro, rows, width), b),
            vm((pay_rows, hw), b),
            vm((pay_rows // 2, hw), b),
            vm((LINE - 1, pay_rows // 2 // LINE, hw), b),
            vm((pay_rows, hw), b),
            vm((width, ff), b),
            vm((ff, width), b),
            vm((width, 256), f),
            vm((256, width), f),
            dma((6,)),
            dma((1 + 4 * micro,)),
            dma((1 + 4 * micro,)),
            dma((2 * micro,)),
            dma((2 * micro,)),
            dma((14,)),
            dma((14,)),
            dma((14,)),
            dma((14,)),
            dma((2 * micro + 4 + cut,)),
        ],
        compiler_params=pltpu.CompilerParams(
            collective_id=0, has_side_effects=True, vmem_limit_bytes=56 * 1024 * 1024
        ),
    )(x, cot, starts, lengths, gain1, wqkv, fmap, wmix, gain2, wup, wdown)

    n = lax.axis_size("dp")
    if n > GROUP:
        same_place = [[i + j * GROUP for j in range(n // GROUP)] for i in range(GROUP)]
        qkv, mix, small, up, down = lax.psum(
            tuple(v.astype(f) for v in (qkv, mix, small, up, down)), "dp", axis_index_groups=same_place
        )
    features = jnp.swapaxes(small[:hs].astype(f).reshape(hs, heads, hs), 0, 1)
    gains = small[hs : hs + 2 * cut].astype(f).reshape(2, width)
    return (
        act,
        ig,
        gains[None, 0],
        qkv.astype(f).reshape(1, 3, width, hw),
        features[None],
        mix.astype(f)[None],
        gains[None, 1],
        up.astype(f)[None],
        down.astype(f)[None],
    )


def solution(mesh):
    in_specs = (
        P(None, ("dp", "mp"), None),
        P(None, ("dp", "mp"), None),
        P(None, "dp", None),
        P(None, "dp", None),
        P("section", None),
        P("section", None, None, "mp"),
        P("section", "mp", None, None),
        P("section", "mp", None),
        P("section", None),
        P("section", None, "mp"),
        P("section", "mp", None),
    )
    out_specs = (
        P("section", None, ("dp", "mp"), None),
        P("section", None, ("dp", "mp"), None),
        P("section", None),
        P("section", None, None, "mp"),
        P("section", "mp", None, None),
        P("section", "mp", None),
        P("section", None),
        P("section", None, "mp"),
        P("section", "mp", None),
    )
    return jax.shard_map(
        on_device, mesh=mesh, in_specs=in_specs, out_specs=out_specs, check_vma=False
    )
```

time: 1210 us -> 205 us (0.17)
  the two profiles are of different devices: /device:TPU:1 before, /device:TPU:20 now
where the time goes in v1:
time: 205 us
  Pallas kernels  189 us (92%)
  other arithmetic  11.8 us (6%)
  local copies, waits for them, and re-layouts  3.35 us (2%)
    pallas_call x1, Pallas kernels, on_device(): pl.pallas_call(kernel, out_shape=[out((1, micro, half, width)), out((1, m...  189 us
    broadcast_in_dim x1, other arithmetic, on_device(): down.astype(f)[None]  4.36 us

profile of v1, /device:TPU:20, one launch (start us, length us, event | category | flops | bytes accessed | tf_op | source)
XLA Modules:
  0.0 205.2 jit_solution(9045091748368969042)
XLA Ops:
  0.6 189.3 %shard_map.178 = (bf16[1,2,64,768]{3,2,1,0:T(8,128)(2,1)}, bf16[1,2,64,768]{3,2,1,0:T(8,128)(2,1)}, bf16[2304,384]{1,0:T(8,128)(2,1)}, bf16[384,768]{1,0:T(8,128...) custom-call(bf16[2,64,768]{2,1,0:T(8,128)(2,1)} %x_in.1, ...), custom_call_target="tpu_custom_call" | custom-call | tf_op jit(solution)/shard_map/pallas_call | solution.py:558
  190.0 0.7 slice_convert_fusion.1
  190.7 0.6 copy.22
  191.3 0.6 copy.23
  191.9 0.8 slice_convert_fusion
  192.7 0.1 reshape.40
  192.8 0.7 copy.21
  193.5 0.0 copy-start
  193.5 4.4 %bitcast_convert_fusion = f32[1,1536,768]{2,1,0:T(8,128)} fusion(bf16[1536,768]{1,0:T(8,128)(2,1)} %get-tuple-element.22), kind=kLoop, calls=%fused_computation | loop fusion | flops 1179648 | bytes 7077888 | tf_op jit(solution)/shard_map/broadcast_in_dim | solution.py:646
  197.8 0.0 copy-done
  197.8 0.0 copy-start.1
  197.8 2.8 %bitcast_convert_fusion.1 = f32[1,768,1536]{2,1,0:T(8,128)} fusion(bf16[768,1536]{1,0:T(8,128)(2,1)S(1)} %copy-done), kind=kLoop, calls=%fused_computation.1 | loop fusion | flops 1179648 | bytes 7077888 | tf_op jit(solution)/shard_map/broadcast_in_dim | solution.py:645
  200.7 0.0 copy-done.1
  200.7 0.0 copy-start.2
  200.7 0.0 copy-start.4
  200.7 0.0 copy-start.3
  200.7 2.0 convert.7
  202.7 0.0 copy-done.2
  202.7 1.1 bitcast_convert_fusion.2
  203.8 0.0 copy-done.4
  203.8 0.7 copy.26
  204.5 0.0 copy-done.3
  204.5 0.7 copy.27
  (1 shorter events, 0.0 us)
Async XLA Ops:
  193.5 4.4 %copy-start = (bf16[768,1536]{1,0:T(8,128)(2,1)S(1)}, bf16[768,1536]{1,0:T(8,128)(2,1)}, u32[]{:S(2)}) copy-start(bf16[768,1536]{1,0:T(8,128)(2,1)} %get-tuple-element.21) | copy-start | bytes 7077892
  197.8 2.8 %copy-start.1 = (bf16[2304,384]{1,0:T(8,128)(2,1)S(1)}, bf16[2304,384]{1,0:T(8,128)(2,1)}, u32[]{:S(2)}) copy-start(bf16[2304,384]{1,0:T(8,128)(2,1)} %get-tuple-element.19) | copy-start | bytes 5308420
  200.7 2.0 copy-start.2
  200.7 3.1 %copy-start.4 = (bf16[1,2,64,768]{3,2,1,0:T(8,128)(2,1)S(1)}, bf16[1,2,64,768]{3,2,1,0:T(8,128)(2,1)}, u32[]{:S(2)}) copy-start(bf16[1,2,64,768]{3,2,1,0:T(8,128)(2,1)} %get-tuple-element.43) | copy-start | bytes 589828
  200.7 3.8 %copy-start.3 = (bf16[1,2,64,768]{3,2,1,0:T(8,128)(2,1)S(1)}, bf16[1,2,64,768]{3,2,1,0:T(8,128)(2,1)}, u32[]{:S(2)}) copy-start(bf16[1,2,64,768]{3,2,1,0:T(8,128)(2,1)} %get-tuple-element.44) | copy-start | bytes 589828

commit v2 on v1

v2 whole, which is shorter than its diff:
```python
import functools

import functools

import jax
import jax.numpy as jnp
from jax import lax
from jax.experimental import pallas as pl
from jax.experimental.pallas import tpu as pltpu
from jax.sharding import PartitionSpec as P

STRETCH = 64
GROUP = 8
LINE = 4
MESH = pl.DeviceIdType.MESH
BF = jnp.bfloat16
F32 = jnp.float32
ANY = pl.BlockSpec(memory_space=pl.ANY)
VM = pl.BlockSpec(memory_space=pltpu.VMEM)
SM = pl.BlockSpec(memory_space=pltpu.SMEM)


def dot(a, b, ca=1, cb=0):
    return lax.dot_general(a, b, (((ca,), (cb,)), ((), ())), preferred_element_type=F32)


def normed(v):
    mean = jnp.mean(v, axis=1, keepdims=True)
    c = v - mean
    rstd = lax.rsqrt(jnp.mean(c * c, axis=1, keepdims=True) + 1e-05)
    return c * rstd, rstd


def norm_back(grad, gain, xhat, rstd):
    t = grad * gain
    mean_t = jnp.mean(t, axis=1, keepdims=True)
    mean_tx = jnp.mean(t * xhat, axis=1, keepdims=True)
    return rstd * (t - mean_t - xhat * mean_tx)


def gelu_both(x):
    k = 0.7978845608028654
    x2 = x * x
    t = jnp.tanh(x * (k + (k * 0.044715) * x2))
    half = 0.5 * (1.0 + t)
    slope = half + 0.5 * x * (1.0 - t * t) * (k + (3.0 * k * 0.044715) * x2)
    return x * half, slope


def both_softmax(logit):
    up = jnp.exp(logit - jnp.max(logit, axis=0, keepdims=True))
    down = jnp.exp(jnp.min(logit, axis=0, keepdims=True) - logit)
    up = up * (1.0 / jnp.sum(up, axis=0, keepdims=True))
    down = down * (1.0 / jnp.sum(down, axis=0, keepdims=True))
    return jnp.concatenate([up.astype(BF), down.astype(BF)], axis=0)


def softmax_back(grad, feat):
    n = grad.shape[0] // 2
    g = grad * feat.astype(F32)
    p = feat.astype(F32)
    one = g[:n] - p[:n] * jnp.sum(g[:n], axis=0, keepdims=True)
    two = g[n:] - p[n:] * jnp.sum(g[n:], axis=0, keepdims=True)
    return one - two


def kernel(
    x_in, cot, starts, lengths, gain1, wqkv_h, fmap, wmix_h, gain2, up_h, down_h,
    act_o, ig_o, qkv_o, mix_o, small_o, up_o, down_o,
    wqkv, wmix, wup, wdown, wupt, rin, gin, mask,
    nrm_t, pt, vnat, qf, kf, st, mt, mtb, den_s, rmid, nm_all, nm_cat, gd_all, hb, gb, gp, part_f, act, igv,
    gbr, gqk, gpt, gacc, sbuf, rbuf,
    ynrm, ymtb, ygpt, ygbr, sb, ysb, hp, fin, from_out, from_opp, from_pair, hnm, hgd,
    lsem, xs, xr, cs, cr, la, ha, fs, us, ys, yr, ars, arr, osem, turn,
):
    s = lax.axis_index("section")
    d = lax.axis_index("dp")
    xi = lax.axis_index("mp")
    micro, half, width = x_in.shape
    rows = 2 * half
    span = micro * rows
    heads, hs = fmap.shape[1], fmap.shape[2]
    hw = heads * hs
    ff = up_h.shape[2]
    g = lax.rem(d, GROUP)
    base = d - g
    pos = lax.div(g, 2)
    par = lax.rem(g, 2)
    to_x = (s, d, 1 - xi)
    to_c = (1 - s, d, xi)
    to_y = (s, base + pos * 2 + 1 - par, xi)
    outer = (pos == 0) | (pos == LINE - 1)
    inner = (pos > 0) & (pos < LINE - 1)
    side = lax.div(pos, 2)
    to_mate = (s, base + (side * 4 + 1 - pos) * 2 + par, xi)
    to_opp = (s, base + (LINE - 1 - pos) * 2 + par, xi)

    def other_core(to):
        return (1 - s,) + to[1:]

    def other_core(to):
        return (1 - s,) + to[1:]

    def at(core, p, q):
        return (core, base + p * 2 + q, xi)

    def greet(act):
        for to in (to_x, to_c, to_y, other_core(to_y)):
            act(to)
        pl.when(pos < LINE - 1)(lambda: act(at(s, pos + 1, par)))
        pl.when(pos > 0)(lambda: act(at(s, pos - 1, par)))

    def local(src, dst, sem):
        return pltpu.make_async_copy(src, dst, sem)

    def remote(src, dst, ss, rs, to):
        return pltpu.make_async_remote_copy(
            src_ref=src, dst_ref=dst, send_sem=ss, recv_sem=rs, device_id=to, device_id_type=MESH
        )

    def cols(m):
        return pl.ds(m * rows, rows)

    def slot(i):
        return pl.ds(pl.multiple_of(i * span, span), span)

    own_x = local(x_in, rin.at[:, pl.ds(0, half)], lsem.at[4])
    own_c = local(cot, gin.at[:, pl.ds(0, half)], lsem.at[4])
    loads = [
        local(wqkv_h.at[0], wqkv, lsem.at[0]),
        local(wmix_h.at[0], wmix, lsem.at[1]),
        local(up_h.at[0], wup, lsem.at[2]),
        local(down_h.at[0], wdown, lsem.at[3]),
    ]

    def first_x(m):
        return remote(rin.at[m, pl.ds(0, half)], rin.at[m, pl.ds(half, half)], xs.at[m], xr.at[m], to_x)

    def first_c(m):
        return remote(gin.at[m, pl.ds(0, half)], gin.at[m, pl.ds(half, half)], xs.at[m], xr.at[m], to_x)

    @pl.when(s == 0)
    def _():
        own_x.start()

    @pl.when(s == 1)
    def _():
        own_c.start()

    for c in loads:
        c.start()

    barrier = pltpu.get_barrier_semaphore()
    greet(lambda to: pl.semaphore_signal(barrier, inc=1, device_id=to, device_id_type=MESH))
    pl.semaphore_wait(barrier, jnp.where(inner, 6, 5))

    @pl.when(s == 0)
    def _():
        own_x.wait()
        first_x(0).start()

    jj = lax.broadcasted_iota(jnp.int32, (rows, rows), 0)
    ii = lax.broadcasted_iota(jnp.int32, (rows, rows), 1)
    j_own, i_own = jj < half, ii < half
    inside = ((j_own == i_own) & (jj <= ii)).astype(F32)
    own_first = jnp.where(xi == 0, 1.0, 0.0)
    across = jnp.where(j_own & ~i_own, own_first, jnp.where(i_own & ~j_own, 1.0 - own_first, 0.0))
    slots = starts.shape[2]
    for m in range(micro):
        n0 = jnp.int32(0)
        n1 = jnp.int32(0)
        for j in range(slots):
            n0 += jnp.where(starts[m, 0, j] <= 0, 1, 0)
            n1 += jnp.where(starts[m, 0, j] <= STRETCH, 1, 0)
        same = jnp.where(n0 == n1, 1.0, 0.0)
        mask[m] = inside + across * same

    def live_of(m, part):
        block = xi if part == 0 else 1 - xi
        begin = jnp.int32(0)
        for j in range(slots):
            begin = jnp.where(starts[m, 0, j] <= block * STRETCH, jnp.maximum(begin, starts[m, 0, j]), begin)
        length = jnp.int32(0)
        for j in range(slots):
            length += jnp.where(starts[m, 0, j] == begin, lengths[m, 0, j], 0)
        row = block * STRETCH + lax.broadcasted_iota(jnp.int32, (half, width), 0)
        return (row - begin < length).astype(F32)

    def block_of(kind, p, q):
        i = p * 2 + q
        return nm_all.at[i] if kind == 0 else gd_all.at[slot(i)]

    class Gather:
        def __init__(self, kind, layer):
            self.kind, self.layer = kind, layer
            self.core = kind
            self.same = layer == kind

        def held(self, p):
            if self.same:
                return block_of(self.kind, p, par)
            return (hnm, hgd)[self.kind].at[p]

        def arrival(self, p):
            return la.at[self.kind, p * 2 + par] if self.same else ha.at[p]

        def send(self, i):
            return fs.at[0 if self.same else 1, i]

        def to(self, core, p, q):
            return (core, base + p * 2 + q, xi)

        def up(self):
            return remote(block_of(self.kind, pos, par), self.held(pos), us.at[0], ha.at[pos], to_c)

        def step(self, i, p, q, ref):
            return remote(ref, self.held(p), self.send(i), self.arrival(p), self.to(self.core, q, par))

        def pair(self, i, p, ref):
            return remote(
                ref, block_of(self.kind, p, par), self.send(i), la.at[self.kind, p * 2 + par], self.to(self.layer, pos, 1 - par)
            )

        def home(self, i, p, ref):
            return remote(
                ref, block_of(self.kind, p, par), self.send(i), la.at[self.kind, p * 2 + par], self.to(self.layer, pos, par)
            )

        def moves(self, way, j):
            p = pos - j if way == 0 else pos + j
            ref = self.held(p)
            i = 3 + (way * (LINE - 1) + j - 1) * 3
            if j == 0:
                return [
                    (self.step(0, p, pos + 1, ref), pos < LINE - 1),
                    (self.step(1, p, pos - 1, ref), pos > 0),
                    (self.pair(2, p, ref), None),
                ]
            came = (p >= 0) if way == 0 else (p < LINE)
            q = pos + 1 if way == 0 else pos - 1
            goes = (q < LINE) if way == 0 else (q >= 0)
            out = [(self.step(i, p, q, ref), came & goes), (self.pair(i + 1, p, ref), came)]
            if not self.same:
                out.append((self.home(i + 2, p, ref), came))
            return out

        def each(self, way, j, what):
            for copy, when in self.moves(way, j):
                if when is None:
                    what(copy)
                else:
                    pl.when(when)(functools.partial(what, copy))

        def own(self):
            if not self.same:
                self.up().wait_recv()
            self.each(0, 0, lambda c: c.start())

        def pass_on(self, j):
            for way in range(2):
                p = pos - j if way == 0 else pos + j

                @pl.when((p >= 0) if way == 0 else (p < LINE))
                def _():
                    self.step(0, p, pos, self.held(p)).wait_recv()

                self.each(way, j, lambda c: c.start())

        def sent(self):
            self.each(0, 0, lambda c: c.wait_send())
            for way in range(2):
                for j in range(1, LINE):
                    self.each(way, j, lambda c: c.wait_send())

        def complete(self):
            for k in range(LINE):
                p = lax.rem(pos + k, LINE)
                ref = block_of(self.kind, p, 1 - par)
                remote(ref, ref, fs.at[0, 0], la.at[self.kind, p * 2 + 1 - par], to_y).wait_recv()
                if k > 0 and not self.same:
                    ref = block_of(self.kind, p, par)
                    remote(ref, ref, fs.at[0, 0], la.at[self.kind, p * 2 + par], to_c).wait_recv()

    nm0, nm1, gd0, gd1 = Gather(0, 0), Gather(0, 1), Gather(1, 0), Gather(1, 1)

    def grad_rows(m):
        return pl.ds(pl.multiple_of(g * span + m * rows, rows), rows)

    @pl.when(s == 0)
    def _():
        first_x(0).wait_recv()
        for m in range(1, micro):
            first_x(m).start()
        pl.semaphore_signal(turn, inc=1, device_id=to_c, device_id_type=MESH)

    @pl.when(s == 1)
    def _():
        for c in loads:
            c.wait()
        wupt[...] = wup[...].T
        own_c.wait()
        pl.semaphore_wait(turn, 1)
        for m in range(micro):
            first_c(m).start()
        for m in range(micro):
            first_c(m).wait_recv()
        for m in range(micro):
            for part in range(2):
                pr = pl.ds(part * half, half)
                to = pl.ds(pl.multiple_of(g * span + m * rows + part * half, half), half)
                gd_all[to] = (gin[m, pr].astype(F32) * live_of(m, part)).astype(BF)
        gd1.own()
        gd1.pass_on(1)

    def x_swap(e, m):
        i = (1 + e) * micro + m
        return remote(sbuf.at[e, m], rbuf.at[e, m], xs.at[i], xr.at[i], to_x)

    def give(e, m, part):
        part = part.astype(BF)
        sbuf[e, m, pl.ds(0, half)] = part[half:]
        sbuf[e, m, pl.ds(half, half)] = part[:half]
        x_swap(e, m).start()

    def c_copy(e, m):
        i = e * micro + m
        src, dst = ((act, rin), (igv, gin))[e]
        return remote(src.at[m], dst.at[m], cs.at[i], cr.at[i], to_c)

    def y_copies(when):
        out = []
        if when == 0:
            pairs = [(nrm_t, ynrm), (mtb, ymtb)]
        else:
            pairs = [
                (gpt.at[1 - par], ygpt.at[0]),
                (gpt.at[2], ygpt.at[1]),
                (gbr.at[:, pl.ds(pl.multiple_of((1 - par) * hw, 128), hw)], ygbr),
                (sb.at[1 - par], ysb),
            ]
        for i, (src, dst) in enumerate(pairs):
            j = 2 * when + i
            out.append(remote(src, dst, ys.at[j], yr.at[j], to_y))
        return out

    def mixer_forward(m):
        @pl.when(s == 0)
        def _():
            if m > 0:
                first_x(m).wait_recv()

        @pl.when(s == 1)
        def _():
            c_copy(0, m).wait_recv()

        if m == 0:
            @pl.when(s == 0)
            def _():
                loads[0].wait()
        r = rin[m].astype(F32)
        n = (normed(r)[0] * gain1[...]).astype(BF)
        nrm_t[:, cols(m)] = n.T
        for q in range(3):
            p = dot(n, wqkv[q]).astype(BF)
            if q == 2:
                vnat[m] = p
            pt[q, :, cols(m)] = p.T
        for h in range(heads):
            hr = pl.ds(h * hs, hs)
            w = fmap[0, h]
            qfh = both_softmax(dot(w, pt[0, hr, cols(m)], 0, 0))
            kfh = both_softmax(dot(w, pt[1, hr, cols(m)], 0, 0))
            qf[m, h] = qfh
            kf[m, h] = kfh
            sc = dot(kfh, qfh, 0, 0) * mask[m]
            den = 1.0 / jnp.sum(sc, axis=0, keepdims=True)
            scb = sc.astype(BF)
            st[m, h] = scb
            den_s[m, h] = jnp.broadcast_to(den, (8, rows))
            mx = dot(pt[2, hr, cols(m)], scb) * den
            mt[m, hr] = mx
            mtb[hr, cols(m)] = mx.astype(BF)
        if m == 0:
            @pl.when(s == 0)
            def _():
                loads[1].wait()
        part = dot(mtb[:, cols(m)].T, wmix[...])
        give(0, m, part)
        rmid[m] = r + part

    def ffn_forward(m):
        x_swap(0, m).wait_recv()
        r = rmid[m] + rbuf[0, m].astype(F32)
        rmid[m] = r
        n = (normed(r)[0] * gain2[...]).astype(BF)
        nm_all[g, :, cols(m)] = n.T
        if m == 0:
            @pl.when(s == 0)
            def _():
                loads[2].wait()
                loads[3].wait()
        h, slope = gelu_both(dot(n, wup[...]))
        h = h.astype(BF)
        gp[m] = slope.astype(BF)
        part = dot(h, wdown[...])
        give(1, m, part)
        part_f[m] = r + part

    def act_copy(m):
        return local(act.at[m, pl.ds(0, half)], act_o.at[0, m], osem.at[m])

    def ig_copy(m):
        return local(igv.at[m, pl.ds(0, half)], ig_o.at[0, m], osem.at[micro + m])

    def end_forward(m):
        x_swap(1, m).wait_recv()
        act[m] = (part_f[m] + rbuf[1, m].astype(F32)).astype(BF)

        @pl.when(s == 0)
        def _():
            c_copy(0, m).start()

        act_copy(m).start()

    for m in range(micro):
        mixer_forward(m)
    @pl.when(s == 1)
    def _():
        gd1.pass_on(2)

    @pl.when(s == 0)
    def _():
        for c in y_copies(0):
            c.start()

    for m in range(micro):
        ffn_forward(m)

    @pl.when(s == 0)
    def _():
        nm0.own()

    @pl.when(s == 1)
    def _():
        nm1.up().start()
        gd1.pass_on(3)

    for m in range(micro):
        end_forward(m)

    tile = 512
    tiles = ff // tile

    def hid_rows(t):
        return pl.ds(pl.multiple_of(t * tile, tile), tile)

    def hidden_ahead(lo, hi, which):
        def one(k, carry):
            i = which(k)
            for t in range(tiles):
                h, slope = gelu_both(dot(wupt[hid_rows(t)], nm_all[i]))
                hb[hid_rows(t), slot(i)] = h.astype(BF)
                gb[hid_rows(t), slot(i)] = slope.astype(BF)
            return carry

        lax.fori_loop(lo, hi, one, 0)

    @pl.when(s == 0)
    def _():
        wupt[...] = wup[...].T
        nm0.pass_on(1)
        hidden_ahead(0, 1, lambda k: g)
        nm0.pass_on(2)
        nm1.own()
        nm0.pass_on(3)
        nm1.pass_on(1)
        hidden_ahead(1, LINE, lambda k: lax.rem(pos + k, LINE) * 2 + par)
        nm1.pass_on(2)
        nm1.pass_on(3)

    def ffn_back(m):
        @pl.when(s == 0)
        def _():
            c_copy(1, m).wait_recv()
            gd_all[grad_rows(m)] = gin[m]

        gd = gd_all[grad_rows(m)]
        gpre = (dot(gd, wdown[...], 1, 1) * gp[m].astype(F32)).astype(BF)
        part = dot(gpre, wup[...], 1, 1)
        give(2, m, part)
        part_f[m] = part

    def mixer_back(m):
        x_swap(2, m).wait_recv()
        gn = part_f[m] + rbuf[2, m].astype(F32)
        xhat, rstd = normed(rmid[m])
        gacc[1, m] = jnp.broadcast_to(jnp.sum(gn * xhat, axis=0, keepdims=True), (8, width))
        gm = gd_all[grad_rows(m)].astype(F32) + norm_back(gn, gain2[...], xhat, rstd)
        rmid[m] = gm
        gb_ = gm.astype(BF)
        gbr[cols(m)] = gb_
        gmt = dot(wmix[...], gb_, 1, 1).astype(BF)
        for h in range(heads):
            hr = pl.ds(h * hs, hs)
            den = den_s[m, h, pl.ds(0, 1)]
            go = gmt[h * hs : (h + 1) * hs].astype(F32)
            gden = -jnp.sum(go * mt[m, hr], axis=0, keepdims=True) * den
            gnum = (go * den).astype(BF)
            pad = jnp.zeros_like(gnum)
            wide = jnp.concatenate([gnum, pad] if h % 2 == 0 else [pad, gnum], axis=0)
            gst = ((dot(vnat[m, :, pl.ds((h // 2) * 2 * hs, 2 * hs)], wide) + gden) * mask[m]).astype(BF)
            qfh = qf[m, h]
            kfh = kf[m, h]
            gql = softmax_back(dot(kfh, gst), qfh).astype(BF)
            gkl = softmax_back(dot(qfh, gst, 1, 1), kfh).astype(BF)
            gv = dot(gnum, st[m, h], 1, 1).astype(BF)
            gqk[0, hr, cols(m)] = gql
            gqk[1, hr, cols(m)] = gkl
            w = fmap[0, h]
            gpt[0, hr, cols(m)] = dot(w, gql).astype(BF)
            gpt[1, hr, cols(m)] = dot(w, gkl).astype(BF)
            gpt[2, hr, cols(m)] = gv
        gnt = dot(wqkv[0], gpt[0, :, cols(m)]) + dot(wqkv[1], gpt[1, :, cols(m)]) + dot(wqkv[2], gpt[2, :, cols(m)])
        part = gnt.T
        give(3, m, part)
        part_f[m] = part

    def end_back(m):
        x_swap(3, m).wait_recv()
        gn = part_f[m] + rbuf[3, m].astype(F32)
        xhat, rstd = normed(rin[m].astype(F32))
        gacc[0, m] = jnp.broadcast_to(jnp.sum(gn * xhat, axis=0, keepdims=True), (8, width))
        igv[m] = (rmid[m] + norm_back(gn, gain1[...], xhat, rstd)).astype(BF)

        @pl.when(s == 1)
        def _():
            c_copy(1, m).start()

        ig_copy(m).start()

    for m in range(micro):
        ffn_back(m)

    @pl.when(s == 0)
    def _():
        gd0.up().start()

    for m in range(micro):
        mixer_back(m)
    late = y_copies(1)

    @pl.when(s == 0)
    def _():
        for c in late[:3]:
            c.start()

    cut = width // hw
    q_rows = pl.ds(0, width)
    v_rows = pl.ds(width, width // 2)
    m_rows = pl.ds(width + width // 2, hw)
    s_rows = pl.ds(width + width // 2 + hw, hs)
    v_part = pl.ds(pl.multiple_of(par * (width // 2), 16), width // 2)
    m_part = pl.ds(pl.multiple_of(par * hw, 128), hw)

    left = lax.broadcasted_iota(jnp.int32, (hs, 2 * hs), 1) < hs
    for p in range(heads // 2):
        pr = pl.ds(p * 2 * hs, 2 * hs)
        tot = dot(pt[0, pr], gqk[0, pr], 1, 1) + dot(pt[1, pr], gqk[1, pr], 1, 1)
        sb[0, :, pr] = jnp.where(left, tot[:hs], tot[hs:]).astype(BF)

    for m in range(micro):
        end_back(m)

    row = lax.broadcasted_iota(jnp.int32, (hs, hw), 0)
    block = jnp.zeros((hs, hw), F32)
    for e in range(2):
        tot = gacc[e, 0, pl.ds(0, 1)]
        for m in range(1, micro):
            tot += gacc[e, m, pl.ds(0, 1)]
        for c in range(cut):
            block = jnp.where(row == e * cut + c, tot[:, c * hw : (c + 1) * hw], block)
    sb[1] = block.astype(BF)

    part_rows = hp.shape[0] // 2
    chunk = part_rows // 4

    class Line:
        def __init__(self, n):
            self.n = n

        def piece(self, near, j):
            group = side if near else 1 - side
            return pl.ds(pl.multiple_of((group * self.n + j) * chunk, 16), chunk)

        def final(self, near, j):
            if self.n == 4:
                return fin.at[self.piece(near, j)]
            group = side if near else 1 - side
            return fin.at[pl.ds(pl.multiple_of(par * part_rows + (group * self.n + j) * chunk, 16), chunk)]

        def send_in(self, near, j):
            i = 4 * near + j
            return remote(hp.at[self.piece(near, j)], from_out.at[i], ars.at[i], arr.at[i], to_mate)

        def send_over(self, j):
            return remote(hp.at[self.piece(0, j)], from_opp.at[j], ars.at[8 + j], arr.at[8 + j], to_opp)

        def total_over(self, j):
            ref = self.final(1, j)
            return remote(ref, ref, ars.at[12 + j], arr.at[12 + j], to_opp)

        def total_out(self, near, j):
            i = 16 + 4 * near + j
            ref = self.final(near, j)
            return remote(ref, ref, ars.at[i], arr.at[i], to_mate)

        def total_pair(self, near, j):
            i = 24 + 4 * near + j
            ref = self.final(near, j)
            return remote(ref, ref, ars.at[i], arr.at[i], to_y)

        def trade(self, j):
            return remote(hp.at[self.piece(1, j)], from_pair.at[j], ars.at[24 + j], arr.at[24 + j], to_y)

        def start(self):
            @pl.when(outer)
            def _():
                for near in range(2):
                    for j in range(self.n):
                        self.send_in(near, j).start()

        def collect(self, j):
            @pl.when(inner)
            def _():
                self.send_in(0, j).wait_recv()
                p = self.piece(0, j)
                hp[p] = (hp[p].astype(F32) + from_out[j].astype(F32)).astype(BF)
                self.send_over(j).start()

        def total(self, j):
            @pl.when(inner)
            def _():
                self.send_in(1, j).wait_recv()
                self.send_over(j).wait_recv()
                p = self.piece(1, j)
                tot = hp[p].astype(F32) + from_out[4 + j].astype(F32) + from_opp[j].astype(F32)
                if self.n == 4:
                    hp[p] = tot.astype(BF)
                    self.trade(j).start()
                else:
                    self.final(1, j)[...] = tot.astype(BF)
                    self.total_out(1, j).start()
                    self.total_over(j).start()

            if self.n == 2:
                @pl.when(outer)
                def _():
                    self.total_out(1, j).wait_recv()

                self.total_pair(1, j).start()

        def settle(self, j):
            @pl.when(inner)
            def _():
                self.trade(j).wait_recv()
                tot = hp[self.piece(1, j)].astype(F32) + from_pair[j].astype(F32)
                self.final(1, j)[...] = tot.astype(BF)
                self.total_out(1, j).start()
                self.total_over(j).start()

            @pl.when(outer)
            def _():
                self.total_out(1, j).wait_recv()

        def passed(self, j):
            @pl.when(inner)
            def _():
                self.total_over(j).wait_recv()
                self.total_out(0, j).start()

            @pl.when(outer)
            def _():
                self.total_out(0, j).wait_recv()

            if self.n == 2:
                self.total_pair(0, j).start()

        def finish(self):
            for j in range(self.n):
                @pl.when(outer)
                def _():
                    self.send_in(0, j).wait_send()
                    self.send_in(1, j).wait_send()

                @pl.when(inner)
                def _():
                    self.send_over(j).wait_send()
                    self.total_over(j).wait_send()
                    self.total_out(0, j).wait_send()
                    self.total_out(1, j).wait_send()
                    if self.n == 4:
                        self.trade(j).wait_send()

                if self.n == 2:
                    self.total_pair(0, j).wait_send()
                    self.total_pair(1, j).wait_send()

    first, second = Line(2), Line(4)

    def joined():
        for i in range(GROUP):
            nm_cat[:, pl.ds(i * span, span)] = nm_all[i]

    def grads_in(t):
        def one(i, carry):
            hr, sl = hid_rows(t), slot(i)
            gb[hr, sl] = (dot(wdown[hr], gd_all[sl], 1, 1) * gb[hr, sl].astype(F32)).astype(BF)
            return carry

        lax.fori_loop(0, GROUP, one, 0, unroll=2)

    def up_copy(t):
        return local(wup.at[:, hid_rows(t)], up_o.at[:, hid_rows(t)], osem.at[2 * micro + 10 + t])

    def down_copy(t):
        return local(wdown.at[hid_rows(t)], down_o.at[hid_rows(t)], osem.at[2 * micro + 10 + tiles + t])

    def grads_up(t):
        wup[:, hid_rows(t)] = dot(nm_cat[...], gb[hid_rows(t)], 1, 1).astype(BF)
        up_copy(t).start()

    def grads_down(t):
        wdown[hid_rows(t)] = dot(hb[hid_rows(t)], gd_all[...]).astype(BF)
        down_copy(t).start()

    @pl.when(s == 0)
    def _():
        late[3].start()
        for c in y_copies(0) + late:
            c.wait_recv()
        hp[q_rows] = (dot(nrm_t[...], gpt[par], 1, 1) + dot(ynrm[...], ygpt[0], 1, 1)).astype(BF)
        hp[v_rows] = (dot(nrm_t[v_part], gpt[2], 1, 1) + dot(ynrm[v_part], ygpt[1], 1, 1)).astype(BF)
        hp[m_rows] = (dot(mtb[...], gbr[:, m_part]) + dot(ymtb[...], ygbr[...])).astype(BF)
        hp[s_rows] = (sb[par].astype(F32) + ysb[...].astype(F32)).astype(BF)
        first.start()
        nm0.complete()

    @pl.when(s == 1)
    def _():
        gd0.own()
        for q in range(3):
            hp[pl.ds(q * width, width)] = dot(nrm_t[...], gpt[q], 1, 1).astype(BF)
        tot = dot(mtb[...], gbr[...]).astype(BF)
        for c in range(cut):
            hp[pl.ds(3 * width + c * hw, hw)] = tot[:, c * hw : (c + 1) * hw]
        for e in range(2):
            hp[pl.ds(3 * width + cut * hw + e * hs, hs)] = sb[e]
        second.start()
        gd0.pass_on(1)
        second.collect(0)
        gd0.pass_on(2)
        second.collect(1)
        nm1.complete()
        gd1.complete()

    hidden_ahead(0, jnp.where(s == 0, LINE, GROUP), lambda k: lax.rem(g + jnp.where(s == 0, 2 * k + 1 - 2 * par, k) + GROUP, GROUP))
    joined()

    @pl.when(s == 0)
    def _():
        first.collect(0)
        first.collect(1)
        gd0.complete()

    @pl.when(s == 1)
    def _():
        gd0.pass_on(3)

    plan = {
        (0, 0): ([], [("collect", 2)]),
        (0, 1): ([("total", 0)], [("collect", 3)]),
        (0, 2): ([], []),
        (1, 0): ([("total", 1)], []),
        (1, 1): ([("passed", 0)], [("total", 0)]),
        (1, 2): ([], [("total", 1)]),
        (2, 0): ([("passed", 1)], [("settle", 0)]),
        (2, 1): ([], [("total", 2), ("settle", 1)]),
        (2, 2): ([], [("total", 3)]),
    }

    def between(t, part):
        for (at_t, at_part), steps in plan.items():
            for layer, line in enumerate((first, second)):
                if at_part == part and steps[layer]:
                    @pl.when((s == layer) & (t == at_t))
                    def _():
                        for name, j in steps[layer]:
                            getattr(line, name)(j)

    def one_tile(t, carry):
        grads_in(t)
        between(t, 0)
        grads_up(t)
        between(t, 1)
        grads_down(t)
        between(t, 2)
        return carry

    lax.fori_loop(0, tiles, one_tile, 0)

    @pl.when(s == 0)
    def _():
        for near in range(2):
            for j in range(2):
                first.total_pair(near, j).wait_recv()

    @pl.when(s == 1)
    def _():
        second.settle(2)
        second.settle(3)
        for j in range(4):
            second.passed(j)

    def outs_of(layer, out_copy):
        if layer == 1:
            out_copy(fin.at[pl.ds(0, 3 * width)], qkv_o)
            for c in range(cut):
                out_copy(fin.at[pl.ds(3 * width + c * hw, hw)], mix_o.at[:, pl.ds(c * hw, hw)])
            for e in range(2):
                out_copy(fin.at[pl.ds(3 * width + cut * hw + e * hs, hs)], small_o.at[e])
            return
        for e in range(2):
            at = e * part_rows
            out_copy(fin.at[pl.ds(at, width)], qkv_o.at[pl.ds(e * width, width)])
            at += width
            out_copy(fin.at[pl.ds(at, width // 2)], qkv_o.at[pl.ds(2 * width + e * (width // 2), width // 2)])
            at += width // 2
            out_copy(fin.at[pl.ds(at, hw)], mix_o.at[:, pl.ds(e * hw, hw)])
            at += hw
            out_copy(fin.at[pl.ds(at, hs)], small_o.at[e])

    def ended(layer):
        mine = []

        def keep(src, dst):
            c = local(src, dst, osem.at[2 * micro + 2 + len(mine)])
            c.start()
            mine.append(c)

        outs_of(layer, keep)
        for c in mine:
            c.wait()

    for t in range(tiles):
        up_copy(t).wait()
        down_copy(t).wait()

    @pl.when(s == 0)
    def _():
        ended(0)

    @pl.when(s == 1)
    def _():
        ended(1)

    @pl.when(s == 0)
    def _():
        for m in range(micro):
            first_x(m).wait_send()
            c_copy(0, m).wait_send()

    @pl.when(s == 1)
    def _():
        for m in range(micro):
            first_c(m).wait_send()
            c_copy(1, m).wait_send()

    for e in range(4):
        for m in range(micro):
            x_swap(e, m).wait_send()
    @pl.when(s == 0)
    def _():
        nm0.sent()
        nm1.sent()
        gd0.up().wait_send()

    @pl.when(s == 1)
    def _():
        gd1.sent()
        gd0.sent()
        nm1.up().wait_send()

    @pl.when(s == 0)
    def _():
        for c in y_copies(0) + y_copies(1):
            c.wait_send()
        first.finish()

    @pl.when(s == 1)
    def _():
        second.finish()

    for m in range(micro):
        act_copy(m).wait()
        ig_copy(m).wait()


def widen(qkv, mix, small, up, down, qkv_o, mix_o, feat_o, g1_o, g2_o, up_o, down_o, sem_in, sem_out, *bufs):
    hs = feat_o.shape[2]
    hw = mix.shape[0]
    cut = mix.shape[1] // hw
    blocks = []
    for src, dst, step in ((up, up_o, 192), (down, down_o, 384), (qkv, qkv_o, 768), (mix, mix_o, 192)):
        for lo in range(0, src.shape[0], step):
            if dst is qkv_o:
                blocks.append((src.at[pl.ds(lo, step)], dst.at[0, lo // step]))
            else:
                blocks.append((src.at[pl.ds(lo, step)], dst.at[0, pl.ds(lo, step)]))
    half = len(blocks)
    narrow, wide = bufs[:half], bufs[half : 2 * half]
    small_v, feat_v, g1_v, g2_v = bufs[2 * half :]
    first = pltpu.make_async_copy(small, small_v, sem_in.at[half])
    first.start()
    loads = [pltpu.make_async_copy(b[0], n, sem_in.at[i]) for i, (b, n) in enumerate(zip(blocks, narrow))]
    for c in loads:
        c.start()
    outs = []

    def put(src, dst, i):
        c = pltpu.make_async_copy(src, dst, sem_out.at[i])
        c.start()
        outs.append(c)

    first.wait()
    for h in range(feat_v.shape[1]):
        feat_v[0, h] = small_v[0, pl.ds(0, hs), pl.ds(h * hs, hs)].astype(F32)
    for c in range(cut):
        cs = pl.ds(c * hw, hw)
        g1_v[:, cs] = small_v[1, pl.ds(0, 16)].astype(F32)[c : c + 1]
        g2_v[:, cs] = small_v[1, pl.ds(0, 16)].astype(F32)[cut + c : cut + c + 1]
    put(feat_v, feat_o, half)
    put(g1_v, g1_o, half + 1)
    put(g2_v, g2_o, half + 2)
    for i, (b, n, w) in enumerate(zip(blocks, narrow, wide)):
        loads[i].wait()
        w[...] = n[...].astype(F32)
        put(w, b[1], i)
    for c in outs:
        c.wait()


def on_device(x, cot, starts, lengths, gain1, wqkv, fmap, wmix, gain2, wup, wdown):
    micro, half, width = x.shape
    rows = 2 * half
    span = micro * rows
    heads, hs = fmap.shape[1], fmap.shape[2]
    hw = heads * hs
    ff = wup.shape[2]
    cut = width // hw
    part_rows = width + width // 2 + hw + hs
    f, b = F32, BF
    vm = pltpu.VMEM
    dma = pltpu.SemaphoreType.DMA
    out = lambda shape, t=b: jax.ShapeDtypeStruct(shape, t)
    act, ig, qkv, mix, small, up, down = pl.pallas_call(
        kernel,
        out_shape=[
            out((1, micro, half, width)),
            out((1, micro, half, width)),
            out((3 * width, hw)),
            out((hw, width)),
            out((2, hs, hw)),
            out((width, ff)),
            out((ff, width)),
        ],
        in_specs=[ANY, ANY, SM, SM, VM, ANY, VM, ANY, VM, ANY, ANY],
        out_specs=[ANY] * 7,
        scratch_shapes=[
            vm((3, width, hw), b),
            vm((hw, width), b),
            vm((width, ff), b),
            vm((ff, width), b),
            vm((ff, width), b),
            vm((micro, rows, width), b),
            vm((micro, rows, width), b),
            vm((micro, rows, rows), f),
            vm((width, span), b),
            vm((3, hw, span), b),
            vm((micro, rows, hw), b),
            vm((micro, heads, 2 * hs, rows), b),
            vm((micro, heads, 2 * hs, rows), b),
            vm((micro, heads, rows, rows), b),
            vm((micro, hw, rows), f),
            vm((hw, span), b),
            vm((micro, heads, 8, rows), f),
            vm((micro, rows, width), f),
            vm((GROUP, width, span), b),
            vm((width, GROUP * span), b),
            vm((GROUP * span, width), b),
            vm((ff, GROUP * span), b),
            vm((ff, GROUP * span), b),
            vm((micro, rows, ff), b),
            vm((micro, rows, width), f),
            vm((micro, rows, width), b),
            vm((micro, rows, width), b),
            vm((span, width), b),
            vm((2, hw, span), b),
            vm((3, hw, span), b),
            vm((2, micro, 8, width), f),
            vm((4, micro, rows, width), b),
            vm((4, micro, rows, width), b),
            vm((width, span), b),
            vm((hw, span), b),
            vm((2, hw, span), b),
            vm((span, hw), b),
            vm((2, hs, hw), b),
            vm((hs, hw), b),
            vm((2 * part_rows, hw), b),
            vm((2 * part_rows, hw), b),
            vm((8, part_rows // 4, hw), b),
            vm((4, part_rows // 4, hw), b),
            vm((4, part_rows // 4, hw), b),
            vm((LINE, width, span), b),
            vm((LINE, span, width), b),
            dma((5,)),
            dma((5 * micro,)),
            dma((5 * micro,)),
            dma((2 * micro,)),
            dma((2 * micro,)),
            dma((2, GROUP)),
            dma((LINE,)),
            dma((2, 21)),
            dma((1,)),
            dma((6,)),
            dma((6,)),
            dma((32,)),
            dma((32,)),
            dma((2 * micro + 16,)),
            pltpu.SemaphoreType.REGULAR,
        ],
        compiler_params=pltpu.CompilerParams(
            collective_id=0, has_side_effects=True, vmem_limit_bytes=60 * 1024 * 1024
        ),
    )(x, cot, starts, lengths, gain1, wqkv, fmap, wmix, gain2, wup, wdown)

    n = lax.axis_size("dp")
    if n > GROUP:
        same_place = [[i + j * GROUP for j in range(n // GROUP)] for i in range(GROUP)]
        qkv, mix, small, up, down = lax.psum((qkv, mix, small, up, down), "dp", axis_index_groups=same_place)

    shapes = []
    for a, step in ((up, 192), (down, 384), (qkv, 768), (mix, 192)):
        shapes += [(step, a.shape[1])] * (a.shape[0] // step)
    outs = [(1, 3, width, hw), (1, hw, width), (1, heads, hs, hs), (1, width), (1, width), (1, width, ff), (1, ff, width)]
    qkv, mix, features, g1, g2, up, down = pl.pallas_call(
        widen,
        out_shape=[out(o, f) for o in outs],
        in_specs=[ANY] * 5,
        out_specs=[ANY] * 7,
        scratch_shapes=[dma((len(shapes) + 1,)), dma((len(shapes) + 3,))]
        + [vm(o, b) for o in shapes]
        + [vm(o, f) for o in shapes]
        + [vm(small.shape, b), vm(outs[2], f), vm(outs[3], f), vm(outs[4], f)],
        compiler_params=pltpu.CompilerParams(vmem_limit_bytes=60 * 1024 * 1024),
    )(qkv, mix, small, up, down)
    return act, ig, g1, qkv, features, mix, g2, up, down


def solution(mesh):
    in_specs = (
        P(None, ("dp", "mp"), None),
        P(None, ("dp", "mp"), None),
        P(None, "dp", None),
        P(None, "dp", None),
        P("section", None),
        P("section", None, None, "mp"),
        P("section", "mp", None, None),
        P("section", "mp", None),
        P("section", None),
        P("section", None, "mp"),
        P("section", "mp", None),
    )
    out_specs = (
        P("section", None, ("dp", "mp"), None),
        P("section", None, ("dp", "mp"), None),
        P("section", None),
        P("section", None, None, "mp"),
        P("section", "mp", None, None),
        P("section", "mp", None),
        P("section", None),
        P("section", None, "mp"),
        P("section", "mp", None),
    )
    return jax.shard_map(
        on_device, mesh=mesh, in_specs=in_specs, out_specs=out_specs, check_vma=False
    )
```

time: 205 us -> 164 us (0.80)
  the two profiles are of different devices: /device:TPU:20 before, /device:TPU:1 now
where the time goes in v2:
time: 164 us
  Pallas kernels  162 us (99%)
    pallas_call x1, Pallas kernels, on_device(): pl.pallas_call(kernel, out_shape=[out((1, micro, half, width)), out((1, m...  155 us
    pallas_call x1, Pallas kernels, on_device(): pl.pallas_call(widen, out_shape=[out(o, f) for o in outs], in_specs=[ANY]...  7.3 us

profile of v2, /device:TPU:1, one launch (start us, length us, event | category | flops | bytes accessed | tf_op | source)
XLA Modules:
  0.0 164.2 jit_solution(10731072722687837592)
XLA Ops:
  0.6 154.8 %shard_map.178 = (bf16[1,2,64,768]{3,2,1,0:T(8,128)(2,1)}, bf16[1,2,64,768]{3,2,1,0:T(8,128)(2,1)}, bf16[2304,384]{1,0:T(8,128)(2,1)}, bf16[384,768]{1,0:T(8,128...) custom-call(bf16[2,64,768]{2,1,0:T(8,128)(2,1)} %x_in.1, ...), custom_call_target="tpu_custom_call" | custom-call | tf_op jit(solution)/shard_map/pallas_call | solution.py:965
  155.5 0.0 copy-start.1
  155.5 0.0 copy-start
  155.5 7.3 %shard_map.179 = (f32[1,3,768,384]{3,2,1,0:T(8,128)}, f32[1,384,768]{2,1,0:T(8,128)}, f32[1,6,64,64]{3,2,1,0:T(8,128)}, f32[1,768]{1,0:T(1,128)}, f32[1,768]{1,0...) custom-call(bf16[2304,384]{1,0:T(8,128)(2,1)} %get-tuple-element.25.qkv, ...), custom_call_target="tpu_custom_call" | custom-call | tf_op jit(solution)/shard_map/pallas_call | solution.py:1055
  162.8 0.0 copy-done.1
  162.8 0.7 copy.22
  163.5 0.0 copy-done
  163.5 0.7 copy.23
Async XLA Ops:
  155.5 7.3 %copy-start.1 = (bf16[1,2,64,768]{3,2,1,0:T(8,128)(2,1)S(1)}, bf16[1,2,64,768]{3,2,1,0:T(8,128)(2,1)}, u32[]{:S(2)}) copy-start(bf16[1,2,64,768]{3,2,1,0:T(8,128)(2,1)} %get-tuple-element.46) | copy-start | bytes 589828
  155.5 8.0 %copy-start = (bf16[1,2,64,768]{3,2,1,0:T(8,128)(2,1)S(1)}, bf16[1,2,64,768]{3,2,1,0:T(8,128)(2,1)}, u32[]{:S(2)}) copy-start(bf16[1,2,64,768]{3,2,1,0:T(8,128)(2,1)} %get-tuple-element.47) | copy-start | bytes 589828

commit v3 on v2

v3 whole, which is shorter than its diff:
```python
import functools

import functools

import jax
import jax.numpy as jnp
from jax import lax
from jax.experimental import pallas as pl
from jax.experimental.pallas import tpu as pltpu
from jax.sharding import PartitionSpec as P

STRETCH = 64
GROUP = 8
LINE = 4
MESH = pl.DeviceIdType.MESH
BF = jnp.bfloat16
F32 = jnp.float32
ANY = pl.BlockSpec(memory_space=pl.ANY)
VM = pl.BlockSpec(memory_space=pltpu.VMEM)
SM = pl.BlockSpec(memory_space=pltpu.SMEM)


def dot(a, b, ca=1, cb=0):
    return lax.dot_general(a, b, (((ca,), (cb,)), ((), ())), preferred_element_type=F32)


def normed(v):
    mean = jnp.mean(v, axis=1, keepdims=True)
    c = v - mean
    rstd = lax.rsqrt(jnp.mean(c * c, axis=1, keepdims=True) + 1e-05)
    return c * rstd, rstd


def norm_back(grad, gain, xhat, rstd):
    t = grad * gain
    mean_t = jnp.mean(t, axis=1, keepdims=True)
    mean_tx = jnp.mean(t * xhat, axis=1, keepdims=True)
    return rstd * (t - mean_t - xhat * mean_tx)


def gelu_both(x):
    k = 0.7978845608028654
    x2 = x * x
    g = 0.5 + 0.5 * jnp.tanh(x * (k + (k * 0.044715) * x2))
    h = x * g
    return h, g + h * (1.0 - g) * (2.0 * k + (6.0 * k * 0.044715) * x2)


def both_softmax(logit):
    up = jnp.exp(logit - jnp.max(logit, axis=0, keepdims=True))
    down = jnp.exp(jnp.min(logit, axis=0, keepdims=True) - logit)
    up = up * (1.0 / jnp.sum(up, axis=0, keepdims=True))
    down = down * (1.0 / jnp.sum(down, axis=0, keepdims=True))
    return jnp.concatenate([up.astype(BF), down.astype(BF)], axis=0)


def softmax_back(grad, feat):
    n = grad.shape[0] // 2
    g = grad * feat.astype(F32)
    p = feat.astype(F32)
    one = g[:n] - p[:n] * jnp.sum(g[:n], axis=0, keepdims=True)
    two = g[n:] - p[n:] * jnp.sum(g[n:], axis=0, keepdims=True)
    return one - two


def kernel(
    x_in, cot, starts, lengths, gain1, wqkv_h, fmap, wmix_h, gain2, up_h, down_h,
    act_o, ig_o, qkv_o, mix_o, small_o, up_o, down_o,
    wqkv, wmix, wup, wdown, wupt, rin, gin, mask,
    nrm_t, pt, vnat, qf, kf, st, mt, mtb, den_s, rmid, nm_all, nm_cat, gd_all, hb, gb, gp, part_f, act, igv,
    gbr, gqk, gpt, gacc, sbuf, rbuf,
    ynrm, ymtb, ygpt, ygbr, sb, ysb, hp, fin, from_out, from_opp, from_pair, hgd, hgw,
    lsem, xs, xr, cs, cr, la, ha, fs, hws, ys, yr, ars, arr, osem, tsem,
):
    s = lax.axis_index("section")
    d = lax.axis_index("dp")
    xi = lax.axis_index("mp")
    micro, half, width = x_in.shape
    rows = 2 * half
    span = micro * rows
    heads, hs = fmap.shape[1], fmap.shape[2]
    hw = heads * hs
    ff = up_h.shape[2]
    g = lax.rem(d, GROUP)
    base = d - g
    pos = lax.div(g, 2)
    par = lax.rem(g, 2)
    to_x = (s, d, 1 - xi)
    to_c = (1 - s, d, xi)
    to_y = (s, base + pos * 2 + 1 - par, xi)
    outer = (pos == 0) | (pos == LINE - 1)
    inner = (pos > 0) & (pos < LINE - 1)
    side = lax.div(pos, 2)
    to_mate = (s, base + (side * 4 + 1 - pos) * 2 + par, xi)
    to_opp = (s, base + (LINE - 1 - pos) * 2 + par, xi)

    def other_core(to):
        return (1 - s,) + to[1:]

    def other_core(to):
        return (1 - s,) + to[1:]

    def at(core, p, q):
        return (core, base + p * 2 + q, xi)

    def greet(act):
        for to in (to_x, to_c, to_y, other_core(to_y)):
            act(to)
        pl.when(pos < LINE - 1)(lambda: act(at(s, pos + 1, par)))
        pl.when(pos > 0)(lambda: act(at(s, pos - 1, par)))

    def local(src, dst, sem):
        return pltpu.make_async_copy(src, dst, sem)

    def remote(src, dst, ss, rs, to):
        return pltpu.make_async_remote_copy(
            src_ref=src, dst_ref=dst, send_sem=ss, recv_sem=rs, device_id=to, device_id_type=MESH
        )

    def cols(m):
        return pl.ds(pl.multiple_of(m * rows, rows), rows)

    def each_micro(f):
        lax.fori_loop(0, micro, lambda m, c: (f(m), c)[1], 0)

    def slot(i):
        return pl.ds(pl.multiple_of(i * span, span), span)

    own_x = local(x_in, rin.at[:, pl.ds(0, half)], lsem.at[4])
    own_c = [local(cot.at[m], gin.at[pl.ds(m * rows, half)], lsem.at[4 + m]) for m in range(micro)]
    loads = [
        local(wqkv_h.at[0], wqkv, lsem.at[0]),
        local(wmix_h.at[0], wmix, lsem.at[1]),
        local(up_h.at[0], wup, lsem.at[2]),
        local(down_h.at[0], wdown, lsem.at[3]),
    ]

    def first_x(m):
        return remote(rin.at[m, pl.ds(0, half)], rin.at[m, pl.ds(half, half)], xs.at[m], xr.at[m], to_x)

    def first_c(m):
        src, dst = gin.at[pl.ds(m * rows, half)], gin.at[pl.ds(m * rows + half, half)]
        return remote(src, dst, xs.at[m], xr.at[m], to_x)

    @pl.when(s == 0)
    def _():
        own_x.start()

    @pl.when(s == 1)
    def _():
        for c in own_c:
            c.start()

    for c in loads:
        c.start()

    barrier = pltpu.get_barrier_semaphore()
    greet(lambda to: pl.semaphore_signal(barrier, inc=1, device_id=to, device_id_type=MESH))
    pl.semaphore_wait(barrier, jnp.where(inner, 6, 5))

    @pl.when(s == 0)
    def _():
        own_x.wait()
        first_x(0).start()

    jj = lax.broadcasted_iota(jnp.int32, (rows, rows), 0)
    ii = lax.broadcasted_iota(jnp.int32, (rows, rows), 1)
    j_own, i_own = jj < half, ii < half
    inside = ((j_own == i_own) & (jj <= ii)).astype(F32)
    own_first = jnp.where(xi == 0, 1.0, 0.0)
    across = jnp.where(j_own & ~i_own, own_first, jnp.where(i_own & ~j_own, 1.0 - own_first, 0.0))
    slots = starts.shape[2]
    for m in range(micro):
        n0 = jnp.int32(0)
        n1 = jnp.int32(0)
        for j in range(slots):
            n0 += jnp.where(starts[m, 0, j] <= 0, 1, 0)
            n1 += jnp.where(starts[m, 0, j] <= STRETCH, 1, 0)
        same = jnp.where(n0 == n1, 1.0, 0.0)
        mask[m] = inside + across * same

    def live_of(m, part):
        block = xi if part == 0 else 1 - xi
        begin = jnp.int32(0)
        for j in range(slots):
            begin = jnp.where(starts[m, 0, j] <= block * STRETCH, jnp.maximum(begin, starts[m, 0, j]), begin)
        length = jnp.int32(0)
        for j in range(slots):
            length += jnp.where(starts[m, 0, j] == begin, lengths[m, 0, j], 0)
        row = block * STRETCH + lax.broadcasted_iota(jnp.int32, (half, width), 0)
        return (row - begin < length).astype(F32)

    def block_of(kind, p, q, m):
        i = p * 2 + q
        return nm_all.at[m, i] if kind == 0 else gd_all.at[pl.ds(pl.multiple_of(i * span + m * rows, rows), rows)]

    class Gather:
        def __init__(self, kind, layer):
            self.kind, self.layer = kind, layer
            self.same = (kind, layer) != (1, 0)
            self.core = layer if self.same else 1

        def held(self, p, m):
            if self.same:
                return block_of(self.kind, p, par, m)
            return hgd.at[p, cols(m)]

        def arrived(self, p, q, m):
            return la.at[self.kind, m, p * 2 + q]

        def arrival(self, p, m):
            return self.arrived(p, par, m) if self.same else ha.at[m, p]

        def sending(self, i, m):
            return fs.at[self.kind if self.same else 2, m, i]

        def to(self, core, p, q):
            return (core, base + p * 2 + q, xi)

        def step(self, i, p, q, m, ref):
            return remote(ref, self.held(p, m), self.sending(i, m), self.arrival(p, m), self.to(self.core, q, par))

        def pair(self, i, p, m, ref):
            to = self.to(self.layer, pos, 1 - par)
            return remote(ref, block_of(self.kind, p, par, m), self.sending(i, m), self.arrived(p, par, m), to)

        def home(self, i, p, m, ref):
            to = self.to(self.layer, pos, par)
            return remote(ref, block_of(self.kind, p, par, m), self.sending(i, m), self.arrived(p, par, m), to)

        def moves(self, way, j, m):
            p = pos - j if way == 0 else pos + j
            i = 3 * p
            if j == 0:
                ref = self.held(p, m) if self.same else igv.at[cols(m)]
                return [
                    (self.step(i, p, pos + 1, m, ref), pos < LINE - 1),
                    (self.step(i + 1, p, pos - 1, m, ref), pos > 0),
                    (self.pair(i + 2, p, m, ref), None),
                ]
            ref = self.held(p, m)
            came = (p >= 0) if way == 0 else (p < LINE)
            q = pos + 1 if way == 0 else pos - 1
            goes = (q < LINE) if way == 0 else (q >= 0)
            out = [(self.step(i, p, q, m, ref), came & goes), (self.pair(i + 1, p, m, ref), came)]
            if not self.same:
                out.append((self.home(i + 2, p, m, ref), came))
            return out

        def each(self, way, j, m, what):
            for copy, when in self.moves(way, j, m):
                if when is None:
                    what(copy)
                else:
                    pl.when(when)(functools.partial(what, copy))

        def own(self, m):
            self.each(0, 0, m, lambda c: c.start())

        def pass_on(self, j, m):
            for way in range(2):
                p = pos - j if way == 0 else pos + j

                @pl.when((p >= 0) if way == 0 else (p < LINE))
                def _():
                    self.step(0, p, pos, m, self.held(p, m)).wait_recv()

                self.each(way, j, m, lambda c: c.start())

        def pass_both(self, j):
            for m in range(micro):
                self.pass_on(j, m)

        def sent(self):
            for m in range(micro):
                self.each(0, 0, m, lambda c: c.wait_send())
                for way in range(2):
                    for j in range(1, LINE):
                        self.each(way, j, m, lambda c: c.wait_send())

        def wide_held(self, p, q, m):
            return block_of(self.kind, p, q, m) if self.same else hgw.at[m - 1, q, p]

        def wide_arrived(self, p, q, m):
            return self.arrived(p, q, m) if self.same else hws.at[m - 1, p * 2 + q]

        def wide(self, j, q, m):
            out = []
            for way in range(2):
                p = pos - j if way == 0 else pos + j
                t = pos + 1 if way == 0 else pos - 1
                when = (t < LINE) if way == 0 else (t >= 0)
                came = (p >= 0) if way == 0 else (p < LINE)
                ref = self.wide_held(p, q, m)
                if j == 0 and q is par and not self.same:
                    ref = igv.at[cols(m)]
                i = 4 * (0 if q is par else 1) + p
                if j == 0 and way == 1:
                    i = 16 + (0 if q is par else 1)
                copy = remote(
                    ref, self.wide_held(p, q, m), self.sending(i, m), self.wide_arrived(p, q, m), self.to(self.core, t, par)
                )
                out.append((copy, when if j == 0 else when & came))
            return out

        def wide_home(self, way, j, q, m):
            p = pos - j if way == 0 else pos + j
            i = 8 + 4 * (0 if q is par else 1) + p
            to = self.to(self.layer, pos, par)
            return remote(self.wide_held(p, q, m), block_of(self.kind, p, q, m), self.sending(i, m), self.arrived(p, q, m), to)

        def wide_pair(self, m):
            ref = block_of(self.kind, pos, par, m) if self.same else igv.at[cols(m)]
            to = self.to(self.core, pos, 1 - par)
            return remote(ref, self.wide_held(pos, par, m), self.sending(18, m), self.wide_arrived(pos, par, m), to)

        def wide_own(self, m):
            for copy, when in self.wide(0, par, m):
                pl.when(when)(copy.start)
            self.wide_pair(m).start()

        def wide_on(self, j, m):
            for q in (par, 1 - par):
                if j == 0 and q is par:
                    continue
                if j == 0:
                    ref = self.wide_held(pos, q, m)
                    remote(ref, ref, fs.at[0, 0, 0], self.wide_arrived(pos, q, m), to_y).wait_recv()
                    if not self.same:
                        self.wide_home(0, 0, q, m).start()
                for way, (copy, when) in enumerate(self.wide(j, q, m)):
                    if j > 0:
                        if self.same:
                            pl.when(when)(copy.wait_recv)
                        else:
                            p = pos - j if way == 0 else pos + j
                            came = (p >= 0) if way == 0 else (p < LINE)
                            pl.when(came)(copy.wait_recv)
                            pl.when(came)(self.wide_home(way, j, q, m).start)
                    pl.when(when)(copy.start)

        def mixed_own(self, m):
            if isinstance(m, int):
                (self.own if m == 0 else self.wide_own)(m)
                return
            pl.when(m == 0)(lambda: self.own(0))
            for n in range(1, micro):
                pl.when(m == n)(functools.partial(self.wide_own, n))

        def mixed_on(self, j):
            self.pass_on(j, 0)
            for m in range(1, micro):
                self.wide_on(j, m)

        def mixed_take(self):
            for k in range(LINE):
                p = lax.rem(pos + k, LINE)
                ref = block_of(self.kind, p, 1 - par, 0)
                remote(ref, ref, fs.at[0, 0, 0], self.arrived(p, 1 - par, 0), to_y).wait_recv()
            for way in range(2):
                for j in range(1, LINE):
                    p = pos - j if way == 0 else pos + j
                    last = (p >= 0) & (pos == LINE - 1) if way == 0 else (p < LINE) & (pos == 0)
                    for m in range(1, micro):
                        for q in (par, 1 - par):
                            ref = block_of(self.kind, p, q, m)
                            come = remote(ref, ref, fs.at[0, 0, 0], self.arrived(p, q, m), to_y)
                            pl.when(last)(come.wait_recv)

        def mixed_sent(self):
            self.each(0, 0, 0, lambda c: c.wait_send())
            for way in range(2):
                for j in range(1, LINE):
                    self.each(way, j, 0, lambda c: c.wait_send())
            for m in range(1, micro):
                self.wide_pair(m).wait_send()
                for j in range(LINE):
                    for q in (par, 1 - par):
                        for way, (copy, when) in enumerate(self.wide(j, q, m)):
                            if j == 0 and q is par:
                                pl.when(when)(copy.wait_send)
                                continue
                            pl.when(when)(copy.wait_send)
                            if self.same or (j == 0 and way == 1):
                                continue
                            p = pos - j if way == 0 else pos + j
                            came = (p >= 0) if way == 0 else (p < LINE)
                            pl.when(came)(self.wide_home(way, j, q, m).wait_send)

        def take(self, i):
            p, q = lax.div(i, 2), lax.rem(i, 2)
            for m in range(micro):
                ref = block_of(self.kind, p, q, m)
                remote(ref, ref, fs.at[0, 0, 0], self.arrived(p, q, m), to_y).wait_recv()

    nm0, nm1, gd0, gd1 = Gather(0, 0), Gather(0, 1), Gather(1, 0), Gather(1, 1)

    def grad_rows(m):
        return pl.ds(pl.multiple_of(g * span + m * rows, rows), rows)

    @pl.when(s == 0)
    def _():
        first_x(0).wait_recv()
        for m in range(1, micro):
            first_x(m).start()

    @pl.when(s == 1)
    def _():
        for c in loads:
            c.wait()
        wupt[...] = wup[...].T
        for c in own_c:
            c.wait()
        for m in range(micro):
            first_c(m).start()
        for m in range(micro):
            first_c(m).wait_recv()
            for part in range(2):
                pr = pl.ds(m * rows + part * half, half)
                to = pl.ds(pl.multiple_of(g * span + m * rows + part * half, half), half)
                gd_all[to] = (gin[pr].astype(F32) * live_of(m, part)).astype(BF)
            gd1.mixed_own(m)
        for m in range(1, micro):
            gd1.wide_on(0, m)
        gd1.mixed_on(1)

    def x_swap(e, m):
        i = (1 + e) * micro + m
        return remote(sbuf.at[e, m], rbuf.at[e, m], xs.at[i], xr.at[i], to_x)

    def give(e, m, part):
        part = part.astype(BF)
        sbuf[e, m, pl.ds(0, half)] = part[half:]
        sbuf[e, m, pl.ds(half, half)] = part[:half]
        x_swap(e, m).start()

    def c_copy(e, m):
        i = e * micro + m
        src, dst = ((act.at[m], rin.at[m]), (igv.at[cols(m)], gin.at[cols(m)]))[e]
        return remote(src, dst, cs.at[i], cr.at[i], to_c)

    def y_copies(when):
        out = []
        if when == 0:
            pairs = [(nrm_t, ynrm), (mtb, ymtb)]
        else:
            pairs = [(sb.at[1 - par], ysb)]
        for i, (src, dst) in enumerate(pairs):
            j = 2 * when + i
            out.append(remote(src, dst, ys.at[j], yr.at[j], to_y))
        return out

    def y_late(i, m):
        src, dst = (
            (gpt.at[1 - par, m], ygpt.at[0, m]),
            (gpt.at[2, m], ygpt.at[1, m]),
            (gbr.at[cols(m), pl.ds(pl.multiple_of((1 - par) * hw, 128), hw)], ygbr.at[cols(m)]),
        )[i]
        j = 3 + i * micro + m
        return remote(src, dst, ys.at[j], yr.at[j], to_y)

    def mixer_forward(m):
        @pl.when((s == 0) & (m > 0))
        def _():
            first_x(m).wait_recv()

        @pl.when(s == 1)
        def _():
            c_copy(0, m).wait_recv()

        @pl.when((s == 0) & (m == 0))
        def _():
            loads[0].wait()
            loads[1].wait()

        r = rin[m].astype(F32)
        n = (normed(r)[0] * gain1[...]).astype(BF)
        pts = []
        for q in range(3):
            p = dot(n, wqkv[q]).astype(BF)
            if q == 2:
                vnat[m] = p
            p = p.T
            pt[q, :, cols(m)] = p
            pts.append([p[h * hs : (h + 1) * hs] for h in range(heads)])
        nrm_t[:, cols(m)] = n.T
        ws = [fmap[0, h] for h in range(heads)]
        logits = [[dot(ws[h], pts[q][h], 0, 0) for h in range(heads)] for q in range(2)]
        feats = [[both_softmax(x) for x in logits[q]] for q in range(2)]
        scores = [dot(feats[1][h], feats[0][h], 0, 0) for h in range(heads)]
        keep = mask[m]
        scores = [x * keep for x in scores]
        dens = [1.0 / jnp.sum(x, axis=0, keepdims=True) for x in scores]
        scores = [x.astype(BF) for x in scores]
        mixed = [dot(pts[2][h], scores[h]) * dens[h] for h in range(heads)]
        for h in range(heads):
            hr = pl.ds(h * hs, hs)
            qf[m, h] = feats[0][h]
            kf[m, h] = feats[1][h]
            st[m, h] = scores[h]
            den_s[m, h] = jnp.broadcast_to(dens[h], (8, rows))
            mt[m, hr] = mixed[h]
            mtb[hr, cols(m)] = mixed[h].astype(BF)
        part = dot(mtb[:, cols(m)].T, wmix[...])
        give(0, m, part)
        rmid[m] = r + part

    def ffn_forward(m):
        x_swap(0, m).wait_recv()
        r = rmid[m] + rbuf[0, m].astype(F32)
        rmid[m] = r
        n = (normed(r)[0] * gain2[...]).astype(BF)
        nm_all[m, g] = n.T

        @pl.when(s == 0)
        def _():
            nm0.mixed_own(m)

        @pl.when(s == 1)
        def _():
            nm1.own(m)

        @pl.when((s == 0) & (m == 0))
        def _():
            loads[2].wait()
            loads[3].wait()

        h, slope = gelu_both(dot(n, wup[...]))
        h = h.astype(BF)
        gp[m] = slope.astype(BF)
        part = dot(h, wdown[...])
        give(1, m, part)
        part_f[m] = r + part

    def act_copy(m):
        return local(act.at[m, pl.ds(0, half)], act_o.at[0, m], osem.at[m])

    def ig_copy(m):
        return local(igv.at[pl.ds(pl.multiple_of(m * rows, half), half)], ig_o.at[0, m], osem.at[micro + m])

    def end_forward(m):
        x_swap(1, m).wait_recv()
        act[m] = (part_f[m] + rbuf[1, m].astype(F32)).astype(BF)

        @pl.when(s == 0)
        def _():
            c_copy(0, m).start()

        act_copy(m).start()

    each_micro(mixer_forward)
    @pl.when(s == 0)
    def _():
        for c in y_copies(0):
            c.start()

    @pl.when(s == 1)
    def _():
        gd1.mixed_on(2)

    each_micro(ffn_forward)
    each_micro(end_forward)

    @pl.when(s == 1)
    def _():
        gd1.mixed_on(3)


    tile = hb.shape[0]
    tiles = ff // tile

    def hid_rows(t):
        return pl.ds(pl.multiple_of(t * tile, tile), tile)

    @pl.when(s == 0)
    def _():
        wupt[...] = wup[...].T

        for m in range(1, micro):
            nm0.wide_on(0, m)
        for j in range(1, LINE):
            nm0.mixed_on(j)

    def ffn_back(m):
        @pl.when(s == 0)
        def _():
            c_copy(1, m).wait_recv()
            gd_all[grad_rows(m)] = gin[cols(m)]

        gd = gd_all[grad_rows(m)]
        gpre = (dot(gd, wdown[...], 1, 1) * gp[m].astype(F32)).astype(BF)
        part = dot(gpre, wup[...], 1, 1)
        give(2, m, part)
        part_f[m] = part

    def mixer_back(m):
        @pl.when((s == 1) & (m == 1))
        def _():
            nm1.pass_both(1)

        x_swap(2, m).wait_recv()
        gn = part_f[m] + rbuf[2, m].astype(F32)
        xhat, rstd = normed(rmid[m])
        gacc[1, m] = jnp.broadcast_to(jnp.sum(gn * xhat, axis=0, keepdims=True), (8, width))
        gm = gd_all[grad_rows(m)].astype(F32) + norm_back(gn, gain2[...], xhat, rstd)
        rmid[m] = gm
        gb_ = gm.astype(BF)
        gbr[cols(m)] = gb_

        @pl.when(s == 0)
        def _():
            y_late(2, m).start()

        gmt = dot(wmix[...], gb_, 1, 1).astype(BF)
        dens = [den_s[m, h, pl.ds(0, 1)] for h in range(heads)]
        gos = [gmt[h * hs : (h + 1) * hs].astype(F32) for h in range(heads)]
        gdens = [-jnp.sum(gos[h] * mt[m, pl.ds(h * hs, hs)], axis=0, keepdims=True) * dens[h] for h in range(heads)]
        gnums = [(gos[h] * dens[h]).astype(BF) for h in range(heads)]
        pad = jnp.zeros_like(gnums[0])
        wide = [jnp.concatenate([x, pad] if h % 2 == 0 else [pad, x], axis=0) for h, x in enumerate(gnums)]
        gsts = [dot(vnat[m, :, pl.ds((h // 2) * 2 * hs, 2 * hs)], wide[h]) + gdens[h] for h in range(heads)]
        keep = mask[m]
        gsts = [(x * keep).astype(BF) for x in gsts]
        qfs = [qf[m, h] for h in range(heads)]
        kfs = [kf[m, h] for h in range(heads)]
        gqf = [dot(kfs[h], gsts[h]) for h in range(heads)]
        gkf = [dot(qfs[h], gsts[h], 1, 1) for h in range(heads)]
        gvs = [dot(gnums[h], st[m, h], 1, 1).astype(BF) for h in range(heads)]
        gql = [softmax_back(gqf[h], qfs[h]).astype(BF) for h in range(heads)]
        gkl = [softmax_back(gkf[h], kfs[h]).astype(BF) for h in range(heads)]
        gpq = [dot(fmap[0, h], gql[h]).astype(BF) for h in range(heads)]
        gpk = [dot(fmap[0, h], gkl[h]).astype(BF) for h in range(heads)]
        for h in range(heads):
            hr = pl.ds(h * hs, hs)
            gqk[0, hr, cols(m)] = gql[h]
            gqk[1, hr, cols(m)] = gkl[h]
            gpt[0, m, hr] = gpq[h]
            gpt[1, m, hr] = gpk[h]
            gpt[2, m, hr] = gvs[h]

        @pl.when(s == 0)
        def _():
            y_late(0, m).start()
            y_late(1, m).start()

        gnt = dot(wqkv[0], gpt[0, m]) + dot(wqkv[1], gpt[1, m]) + dot(wqkv[2], gpt[2, m])
        part = gnt.T
        give(3, m, part)
        part_f[m] = part

    def end_back(m):
        x_swap(3, m).wait_recv()
        gn = part_f[m] + rbuf[3, m].astype(F32)
        xhat, rstd = normed(rin[m].astype(F32))
        gacc[0, m] = jnp.broadcast_to(jnp.sum(gn * xhat, axis=0, keepdims=True), (8, width))
        igv[cols(m)] = (rmid[m] + norm_back(gn, gain1[...], xhat, rstd)).astype(BF)

        @pl.when(s == 1)
        def _():
            c_copy(1, m).start()
            gd0.mixed_own(m)

        ig_copy(m).start()

    each_micro(ffn_back)

    each_micro(mixer_back)

    late = y_copies(1)

    cut = width // hw
    q_rows = pl.ds(0, width)
    v_rows = pl.ds(width, width // 2)
    m_rows = pl.ds(width + width // 2, hw)
    s_rows = pl.ds(width + width // 2 + hw, hs)
    v_part = pl.ds(pl.multiple_of(par * (width // 2), 16), width // 2)
    m_part = pl.ds(pl.multiple_of(par * hw, 128), hw)

    left = lax.broadcasted_iota(jnp.int32, (hs, 2 * hs), 1) < hs
    for p in range(heads // 2):
        pr = pl.ds(p * 2 * hs, 2 * hs)
        tot = dot(pt[0, pr], gqk[0, pr], 1, 1) + dot(pt[1, pr], gqk[1, pr], 1, 1)
        sb[0, :, pr] = jnp.where(left, tot[:hs], tot[hs:]).astype(BF)

    each_micro(end_back)

    row = lax.broadcasted_iota(jnp.int32, (hs, hw), 0)
    block = jnp.zeros((hs, hw), F32)
    for e in range(2):
        tot = gacc[e, 0, pl.ds(0, 1)]
        for m in range(1, micro):
            tot += gacc[e, m, pl.ds(0, 1)]
        for c in range(cut):
            block = jnp.where(row == e * cut + c, tot[:, c * hw : (c + 1) * hw], block)
    sb[1] = block.astype(BF)

    part_rows = hp.shape[0] // 2
    chunk = part_rows // 4

    class Line:
        def __init__(self, n):
            self.n = n

        def piece(self, near, j):
            group = side if near else 1 - side
            return pl.ds(pl.multiple_of((group * self.n + j) * chunk, 16), chunk)

        def final(self, near, j):
            if self.n == 4:
                return fin.at[self.piece(near, j)]
            group = side if near else 1 - side
            return fin.at[pl.ds(pl.multiple_of(par * part_rows + (group * self.n + j) * chunk, 16), chunk)]

        def send_in(self, near, j):
            i = 4 * near + j
            return remote(hp.at[self.piece(near, j)], from_out.at[i], ars.at[i], arr.at[i], to_mate)

        def send_over(self, j):
            return remote(hp.at[self.piece(0, j)], from_opp.at[j], ars.at[j], arr.at[8 + j], to_opp)

        def total_over(self, j):
            ref = self.final(1, j)
            return remote(ref, ref, ars.at[4 + j], arr.at[12 + j], to_opp)

        def total_out(self, near, j):
            i = 4 * near + j
            ref = self.final(near, j)
            return remote(ref, ref, ars.at[8 + i], arr.at[i], to_mate)

        def total_pair(self, near, j):
            i = 16 + 2 * near + j if self.n == 2 else 8 + 4 * near + j
            ref = self.final(near, j)
            return remote(ref, ref, ars.at[i], arr.at[i], to_y)

        def trade(self, j):
            return remote(hp.at[self.piece(1, j)], from_pair.at[j], ars.at[16 + j], arr.at[16 + j], to_y)

        def start(self, lo, hi):
            @pl.when(outer)
            def _():
                for j in range(lo, hi):
                    for near in range(2):
                        self.send_in(near, j).start()

        def collect(self, j):
            @pl.when(inner)
            def _():
                self.send_in(0, j).wait_recv()
                p = self.piece(0, j)
                hp[p] = (hp[p].astype(F32) + from_out[j].astype(F32)).astype(BF)
                self.send_over(j).start()

        def total(self, j):
            @pl.when(inner)
            def _():
                self.send_in(1, j).wait_recv()
                self.send_over(j).wait_recv()
                p = self.piece(1, j)
                tot = hp[p].astype(F32) + from_out[4 + j].astype(F32) + from_opp[j].astype(F32)
                if self.n == 4:
                    hp[p] = tot.astype(BF)
                    self.trade(j).start()
                else:
                    self.final(1, j)[...] = tot.astype(BF)
                    self.total_out(1, j).start()
                    self.total_over(j).start()

            if self.n == 2:
                @pl.when(outer)
                def _():
                    self.total_out(1, j).wait_recv()

                self.total_pair(1, j).start()

        def settle(self, j):
            @pl.when(inner)
            def _():
                self.trade(j).wait_recv()
                tot = hp[self.piece(1, j)].astype(F32) + from_pair[j].astype(F32)
                self.final(1, j)[...] = tot.astype(BF)
                self.total_out(1, j).start()
                self.total_over(j).start()

            self.across(1, j)

        def across(self, near, j):
            @pl.when(outer)
            def _():
                self.total_out(near, j).wait_recv()

        def passed(self, j):
            @pl.when(inner)
            def _():
                self.total_over(j).wait_recv()
                self.total_out(0, j).start()

            if self.n == 2:
                @pl.when(outer)
                def _():
                    self.total_out(0, j).wait_recv()

                self.total_pair(0, j).start()
            else:
                self.across(0, j)

        def last(self):
            if self.n == 2:
                for near in range(2):
                    for j in range(2):
                        self.total_pair(near, j).wait_recv()
                return

        def finish(self):
            for j in range(self.n):
                @pl.when(outer)
                def _():
                    self.send_in(0, j).wait_send()
                    self.send_in(1, j).wait_send()

                @pl.when(inner)
                def _():
                    self.send_over(j).wait_send()
                    self.total_over(j).wait_send()
                    if self.n == 4:
                        self.trade(j).wait_send()

                mine = par == j % 2
                for near in range(2):
                    pl.when(inner)(self.total_out(near, j).wait_send)
                    if self.n == 2:
                        self.total_pair(near, j).wait_send()

    first, second = Line(2), Line(4)

    @pl.when(s == 0)
    def _():
        late[0].start()
        for c in y_copies(0) + late:
            c.wait_recv()
        for m in range(micro):
            for i in range(3):
                y_late(i, m).wait_recv()
        q_tot = 0.0
        v_tot = 0.0
        for m in range(micro):
            q_tot += dot(nrm_t[:, cols(m)], gpt[par, m], 1, 1) + dot(ynrm[:, cols(m)], ygpt[0, m], 1, 1)
            v_tot += dot(nrm_t[v_part, cols(m)], gpt[2, m], 1, 1) + dot(ynrm[v_part, cols(m)], ygpt[1, m], 1, 1)
        hp[q_rows] = q_tot.astype(BF)
        hp[v_rows] = v_tot.astype(BF)
        hp[m_rows] = (dot(mtb[...], gbr[:, m_part]) + dot(ymtb[...], ygbr[...])).astype(BF)
        hp[s_rows] = (sb[par].astype(F32) + ysb[...].astype(F32)).astype(BF)
        first.start(0, 2)

    @pl.when(s == 1)
    def _():
        for q in range(3):
            tot = dot(nrm_t[:, cols(0)], gpt[q, 0], 1, 1)
            for m in range(1, micro):
                tot += dot(nrm_t[:, cols(m)], gpt[q, m], 1, 1)
            hp[pl.ds(q * width, width)] = tot.astype(BF)
        tot = dot(mtb[...], gbr[...]).astype(BF)
        for c in range(cut):
            hp[pl.ds(3 * width + c * hw, hw)] = tot[:, c * hw : (c + 1) * hw]
        for e in range(2):
            hp[pl.ds(3 * width + cut * hw + e * hs, hs)] = sb[e]
        for m in range(1, micro):
            gd0.wide_on(0, m)
        second.start(0, 2)
        gd0.mixed_on(1)
        nm1.pass_both(2)
        gd0.mixed_on(2)
        nm1.pass_both(3)
        gd1.mixed_take()

    @pl.when(s == 0)
    def _():
        nm0.mixed_take()
        for k in range(1, GROUP):
            gd0.take(lax.rem(g + k, GROUP))
        first.collect(0)

    @pl.when(s == 1)
    def _():
        second.collect(0)
        gd0.mixed_on(3)
        for k in range(1, GROUP, 2):
            nm1.take(lax.rem(g + k, GROUP))

    def up_copy(t):
        return local(wup.at[:, hid_rows(t)], up_o.at[:, hid_rows(t)], tsem.at[0, t])

    def down_copy(t):
        return local(wdown.at[hid_rows(t)], down_o.at[hid_rows(t)], tsem.at[1, t])

    for i in range(GROUP):
        for m in range(micro):
            nm_cat[:, pl.ds(i * span + m * rows, rows)] = nm_all[m, i]

    def tile_grads(t):
        hr = hid_rows(t)
        wu = wupt[hr]
        wd = wdown[hr]
        for i in range(GROUP):
            sl = slot(i)
            h, slope = gelu_both(dot(wu, nm_cat[:, sl]))
            hb[:, sl] = h.astype(BF)
            gb[:, sl] = (dot(wd, gd_all[sl], 1, 1) * slope).astype(BF)
        wup[:, hr] = dot(nm_cat[...], gb[...], 1, 1).astype(BF)
        wdown[hr] = dot(hb[...], gd_all[...]).astype(BF)
        up_copy(t).start()
        down_copy(t).start()

    plan = {
        (0, True): {
            0: [("total", 0)],
            1: [("collect", 1)],
            2: [("passed", 0), ("total", 1)],
            3: [("passed", 1)],
        },
        (0, False): {2: [("total", 0)], 3: [("passed", 0), ("total", 1)], 4: [("passed", 1)]},
        (1, True): {
            0: [("total", 0), ("collect", 1)],
            1: [("total", 1)],
            2: [("settle", 0)],
            3: [("settle", 1), ("collect", 2)],
            4: [("passed", 0), ("total", 2), ("collect", 3)],
            5: [
                ("passed", 1),
                ("settle", 2),
                ("total", 3),
                ("passed", 2),
                ("settle", 3),
                ("passed", 3),
            ],
        },
        (1, False): {
            0: [("start", 2, 4)],
            5: [(f, j) for j in range(4) for f in ("settle", "passed")],
        },
    }

    def one_tile(t, carry):
        tile_grads(t)
        for (layer, within), when in plan.items():
            for at, steps in when.items():
                @pl.when((s == layer) & (inner if within else outer) & (t == at))
                def _():
                    for name, *j in steps:
                        getattr((first, second)[layer], name)(*j)

        return carry

    lax.fori_loop(0, tiles, one_tile, 0)

    @pl.when(s == 0)
    def _():
        first.last()

    @pl.when(s == 1)
    def _():
        second.last()

    def outs_of(layer, out_copy):
        if layer == 1:
            out_copy(fin.at[pl.ds(0, 3 * width)], qkv_o)
            for c in range(cut):
                out_copy(fin.at[pl.ds(3 * width + c * hw, hw)], mix_o.at[:, pl.ds(c * hw, hw)])
            for e in range(2):
                out_copy(fin.at[pl.ds(3 * width + cut * hw + e * hs, hs)], small_o.at[e])
            return
        for e in range(2):
            at = e * part_rows
            out_copy(fin.at[pl.ds(at, width)], qkv_o.at[pl.ds(e * width, width)])
            at += width
            out_copy(fin.at[pl.ds(at, width // 2)], qkv_o.at[pl.ds(2 * width + e * (width // 2), width // 2)])
            at += width // 2
            out_copy(fin.at[pl.ds(at, hw)], mix_o.at[:, pl.ds(e * hw, hw)])
            at += hw
            out_copy(fin.at[pl.ds(at, hs)], small_o.at[e])

    def ended(layer):
        mine = []

        def keep(src, dst):
            c = local(src, dst, osem.at[2 * micro + 2 + len(mine)])
            c.start()
            mine.append(c)

        outs_of(layer, keep)
        for c in mine:
            c.wait()

    for t in range(tiles):
        up_copy(t).wait()
        down_copy(t).wait()

    @pl.when(s == 0)
    def _():
        ended(0)

    @pl.when(s == 1)
    def _():
        ended(1)

    @pl.when(s == 0)
    def _():
        for m in range(micro):
            first_x(m).wait_send()
            c_copy(0, m).wait_send()

    @pl.when(s == 1)
    def _():
        for m in range(micro):
            first_c(m).wait_send()
            c_copy(1, m).wait_send()

    for e in range(4):
        for m in range(micro):
            x_swap(e, m).wait_send()
    @pl.when(s == 0)
    def _():
        nm0.mixed_sent()

    @pl.when(s == 1)
    def _():
        gd1.mixed_sent()
        gd0.mixed_sent()
        nm1.sent()

    @pl.when(s == 0)
    def _():
        for c in y_copies(0) + y_copies(1):
            c.wait_send()
        for m in range(micro):
            for i in range(3):
                y_late(i, m).wait_send()
        first.finish()

    @pl.when(s == 1)
    def _():
        second.finish()

    for m in range(micro):
        act_copy(m).wait()
        ig_copy(m).wait()


def widen(act, ig, qkv, mix, small, up, down, act_o, ig_o, qkv_o, mix_o, feat_o, g1_o, g2_o, up_o, down_o, sem_in, sem_out, *bufs):
    hs = feat_o.shape[2]
    hw = mix.shape[0]
    cut = mix.shape[1] // hw
    blocks = []
    for src, dst, step in ((up, up_o, 192), (down, down_o, 384), (qkv, qkv_o, 768), (mix, mix_o, 192)):
        for lo in range(0, src.shape[0], step):
            if dst is qkv_o:
                blocks.append((src.at[pl.ds(lo, step)], dst.at[0, lo // step]))
            else:
                blocks.append((src.at[pl.ds(lo, step)], dst.at[0, pl.ds(lo, step)]))
    half = len(blocks)
    narrow, wide = bufs[:half], bufs[half : 2 * half]
    small_v, feat_v, g1_v, g2_v, act_v, ig_v = bufs[2 * half :]
    first = [
        pltpu.make_async_copy(src, dst, sem_in.at[half + i])
        for i, (src, dst) in enumerate(((small, small_v), (act, act_v), (ig, ig_v)))
    ]
    for c in first:
        c.start()
    loads = [pltpu.make_async_copy(b[0], n, sem_in.at[i]) for i, (b, n) in enumerate(zip(blocks, narrow))]
    for c in loads:
        c.start()
    outs = []

    def put(src, dst, i):
        c = pltpu.make_async_copy(src, dst, sem_out.at[i])
        c.start()
        outs.append(c)

    for c in first:
        c.wait()
    put(act_v, act_o, half + 3)
    put(ig_v, ig_o, half + 4)
    for h in range(feat_v.shape[1]):
        feat_v[0, h] = small_v[0, pl.ds(0, hs), pl.ds(h * hs, hs)].astype(F32)
    for c in range(cut):
        cs = pl.ds(c * hw, hw)
        g1_v[:, cs] = small_v[1, pl.ds(0, 16)].astype(F32)[c : c + 1]
        g2_v[:, cs] = small_v[1, pl.ds(0, 16)].astype(F32)[cut + c : cut + c + 1]
    put(feat_v, feat_o, half)
    put(g1_v, g1_o, half + 1)
    put(g2_v, g2_o, half + 2)
    for i, (b, n, w) in enumerate(zip(blocks, narrow, wide)):
        loads[i].wait()
        w[...] = n[...].astype(F32)
        put(w, b[1], i)
    for c in outs:
        c.wait()


def on_device(x, cot, starts, lengths, gain1, wqkv, fmap, wmix, gain2, wup, wdown):
    micro, half, width = x.shape
    rows = 2 * half
    span = micro * rows
    heads, hs = fmap.shape[1], fmap.shape[2]
    hw = heads * hs
    ff = wup.shape[2]
    cut = width // hw
    part_rows = width + width // 2 + hw + hs
    f, b = F32, BF
    vm = pltpu.VMEM
    dma = pltpu.SemaphoreType.DMA
    out = lambda shape, t=b: jax.ShapeDtypeStruct(shape, t)
    act, ig, qkv, mix, small, up, down = pl.pallas_call(
        kernel,
        out_shape=[
            out((1, micro, half, width)),
            out((1, micro, half, width)),
            out((3 * width, hw)),
            out((hw, width)),
            out((2, hs, hw)),
            out((width, ff)),
            out((ff, width)),
        ],
        in_specs=[ANY, ANY, SM, SM, VM, ANY, VM, ANY, VM, ANY, ANY],
        out_specs=[ANY] * 7,
        scratch_shapes=[
            vm((3, width, hw), b),
            vm((hw, width), b),
            vm((width, ff), b),
            vm((ff, width), b),
            vm((ff, width), b),
            vm((micro, rows, width), b),
            vm((span, width), b),
            vm((micro, rows, rows), f),
            vm((width, span), b),
            vm((3, hw, span), b),
            vm((micro, rows, hw), b),
            vm((micro, heads, 2 * hs, rows), b),
            vm((micro, heads, 2 * hs, rows), b),
            vm((micro, heads, rows, rows), b),
            vm((micro, hw, rows), f),
            vm((hw, span), b),
            vm((micro, heads, 8, rows), f),
            vm((micro, rows, width), f),
            vm((micro, GROUP, width, rows), b),
            vm((width, GROUP * span), b),
            vm((GROUP * span, width), b),
            vm((256, GROUP * span), b),
            vm((256, GROUP * span), b),
            vm((micro, rows, ff), b),
            vm((micro, rows, width), f),
            vm((micro, rows, width), b),
            vm((span, width), b),
            vm((span, width), b),
            vm((2, hw, span), b),
            vm((3, micro, hw, rows), b),
            vm((2, micro, 8, width), f),
            vm((4, micro, rows, width), b),
            vm((4, micro, rows, width), b),
            vm((width, span), b),
            vm((hw, span), b),
            vm((2, micro, hw, rows), b),
            vm((span, hw), b),
            vm((2, hs, hw), b),
            vm((hs, hw), b),
            vm((2 * part_rows, hw), b),
            vm((2 * part_rows, hw), b),
            vm((8, part_rows // 4, hw), b),
            vm((4, part_rows // 4, hw), b),
            vm((4, part_rows // 4, hw), b),
            vm((LINE, span, width), b),
            vm((micro - 1, 2, LINE, rows, width), b),
            dma((4 + micro,)),
            dma((5 * micro,)),
            dma((5 * micro,)),
            dma((2 * micro,)),
            dma((2 * micro,)),
            dma((2, micro, GROUP)),
            dma((micro, LINE)),
            dma((3, micro, 20)),
            dma((micro - 1, GROUP)),
            dma((3 + 3 * micro,)),
            dma((3 + 3 * micro,)),
            dma((20,)),
            dma((20,)),
            dma((2 * micro + 10,)),
            dma((2, ff // 256)),
        ],
        compiler_params=pltpu.CompilerParams(
            collective_id=0, has_side_effects=True, vmem_limit_bytes=60 * 1024 * 1024
        ),
    )(x, cot, starts, lengths, gain1, wqkv, fmap, wmix, gain2, wup, wdown)

    n = lax.axis_size("dp")
    if n > GROUP:
        same_place = [[i + j * GROUP for j in range(n // GROUP)] for i in range(GROUP)]
        qkv, mix, small, up, down = lax.psum((qkv, mix, small, up, down), "dp", axis_index_groups=same_place)

    shapes = []
    for a, step in ((up, 192), (down, 384), (qkv, 768), (mix, 192)):
        shapes += [(step, a.shape[1])] * (a.shape[0] // step)
    outs = [(1, 3, width, hw), (1, hw, width), (1, heads, hs, hs), (1, width), (1, width), (1, width, ff), (1, ff, width)]
    act, ig, qkv, mix, features, g1, g2, up, down = pl.pallas_call(
        widen,
        out_shape=[out(act.shape), out(ig.shape)] + [out(o, f) for o in outs],
        in_specs=[ANY] * 7,
        out_specs=[ANY] * 9,
        scratch_shapes=[dma((len(shapes) + 3,)), dma((len(shapes) + 5,))]
        + [vm(o, b) for o in shapes]
        + [vm(o, f) for o in shapes]
        + [vm(small.shape, b), vm(outs[2], f), vm(outs[3], f), vm(outs[4], f), vm(act.shape, b), vm(ig.shape, b)],
        compiler_params=pltpu.CompilerParams(vmem_limit_bytes=60 * 1024 * 1024),
    )(act, ig, qkv, mix, small, up, down)
    return act, ig, g1, qkv, features, mix, g2, up, down


def solution(mesh):
    in_specs = (
        P(None, ("dp", "mp"), None),
        P(None, ("dp", "mp"), None),
        P(None, "dp", None),
        P(None, "dp", None),
        P("section", None),
        P("section", None, None, "mp"),
        P("section", "mp", None, None),
        P("section", "mp", None),
        P("section", None),
        P("section", None, "mp"),
        P("section", "mp", None),
    )
    out_specs = (
        P("section", None, ("dp", "mp"), None),
        P("section", None, ("dp", "mp"), None),
        P("section", None),
        P("section", None, None, "mp"),
        P("section", "mp", None, None),
        P("section", "mp", None),
        P("section", None),
        P("section", None, "mp"),
        P("section", "mp", None),
    )
    return jax.shard_map(
        on_device, mesh=mesh, in_specs=in_specs, out_specs=out_specs, check_vma=False
    )
```

time: 164 us -> 148 us (0.902)
  Pallas kernels: 162 us -> 147 us
    pallas_call x1, Pallas kernels: 155 us -> 139 us  [on_device(): pl.pallas_call(kernel, out_shape=[out((1, micro, half, width)), out((1, m...]
where the time goes in v3:
time: 148 us; the launch traced here: 147 us
  Pallas kernels  147 us (99%)
    pallas_call x1, Pallas kernels, on_device(): pl.pallas_call(kernel, out_shape=[out((1, micro, half, width)), out((1, m...  139 us
    pallas_call x1, Pallas kernels, on_device(): pl.pallas_call(widen, out_shape=[out(act.shape), out(ig.shape)] + [out(o,...  7.5 us

profile of v3, /device:TPU:1, one launch (start us, length us, event | category | flops | bytes accessed | tf_op | source)
XLA Modules:
  0.0 147.4 jit_solution(2785764930070615383)
XLA Ops:
  0.6 139.1 %shard_map.178 = (bf16[1,2,64,768]{3,2,1,0:T(8,128)(2,1)}, bf16[1,2,64,768]{3,2,1,0:T(8,128)(2,1)}, bf16[2304,384]{1,0:T(8,128)(2,1)}, bf16[384,768]{1,0:T(8,128...) custom-call(bf16[2,64,768]{2,1,0:T(8,128)(2,1)} %x_in.1, ...), custom_call_target="tpu_custom_call" | custom-call | tf_op jit(solution)/shard_map/pallas_call | solution.py:1112
  139.8 7.5 %shard_map.179 = (bf16[1,2,64,768]{3,2,1,0:T(8,128)(2,1)}, bf16[1,2,64,768]{3,2,1,0:T(8,128)(2,1)}, f32[1,3,768,384]{3,2,1,0:T(8,128)}, f32[1,384,768]{2,1,0:T(8...) custom-call(bf16[1,2,64,768]{3,2,1,0:T(8,128)(2,1)} %get-tuple-eleme, ...), custom_call_target="tpu_custom_call" | custom-call | tf_op jit(solution)/shard_map/pallas_call | solution.py:1202

commit v4 on v3

--- a/solution.py
+++ b/solution.py
@@ -67,7 +67,7 @@
     x_in, cot, starts, lengths, gain1, wqkv_h, fmap, wmix_h, gain2, up_h, down_h,
     act_o, ig_o, qkv_o, mix_o, small_o, up_o, down_o,
     wqkv, wmix, wup, wdown, wupt, rin, gin, mask,
-    nrm_t, pt, vnat, qf, kf, st, mt, mtb, den_s, rmid, nm_all, nm_cat, gd_all, hb, gb, gp, part_f, act, igv,
+    nrm_t, pt, vnat, qf, kf, st, mt, mtb, den_s, rmid, nm_all, nm_cat, gd_all, hb, gb, gp, part_f, rout, act, igv,
     gbr, gqk, gpt, gacc, sbuf, rbuf,
     ynrm, ymtb, ygpt, ygbr, sb, ysb, hp, fin, from_out, from_opp, from_pair, hgd, hgw,
     lsem, xs, xr, cs, cr, la, ha, fs, hws, ys, yr, ars, arr, osem, tsem,
@@ -195,8 +195,9 @@
         return nm_all.at[m, i] if kind == 0 else gd_all.at[pl.ds(pl.multiple_of(i * span + m * rows, rows), rows)]
 
     class Gather:
-        def __init__(self, kind, layer):
+        def __init__(self, kind, layer, plain):
             self.kind, self.layer = kind, layer
+            self.plain = plain
             self.same = (kind, layer) != (1, 0)
             self.core = layer if self.same else 1
 
@@ -267,22 +268,11 @@
 
                 self.each(way, j, m, lambda c: c.start())
 
-        def pass_both(self, j):
-            for m in range(micro):
-                self.pass_on(j, m)
-
-        def sent(self):
-            for m in range(micro):
-                self.each(0, 0, m, lambda c: c.wait_send())
-                for way in range(2):
-                    for j in range(1, LINE):
-                        self.each(way, j, m, lambda c: c.wait_send())
-
         def wide_held(self, p, q, m):
-            return block_of(self.kind, p, q, m) if self.same else hgw.at[m - 1, q, p]
+            return block_of(self.kind, p, q, m) if self.same else hgw.at[m, q, p]
 
         def wide_arrived(self, p, q, m):
-            return self.arrived(p, q, m) if self.same else hws.at[m - 1, p * 2 + q]
+            return self.arrived(p, q, m) if self.same else hws.at[m, p * 2 + q]
 
         def wide(self, j, q, m):
             out = []
@@ -341,47 +331,48 @@
 
         def mixed_own(self, m):
             if isinstance(m, int):
-                (self.own if m == 0 else self.wide_own)(m)
+                (self.own if m < self.plain else self.wide_own)(m)
                 return
-            pl.when(m == 0)(lambda: self.own(0))
-            for n in range(1, micro):
-                pl.when(m == n)(functools.partial(self.wide_own, n))
+            for n in range(micro):
+                pl.when(m == n)(functools.partial(self.mixed_own, n))
+
+        def crossed(self):
+            for m in range(self.plain, micro):
+                self.wide_on(0, m)
 
         def mixed_on(self, j):
-            self.pass_on(j, 0)
-            for m in range(1, micro):
-                self.wide_on(j, m)
+            for m in range(micro):
+                (self.pass_on if m < self.plain else self.wide_on)(j, m)
 
         def mixed_take(self):
-            for k in range(LINE):
-                p = lax.rem(pos + k, LINE)
-                ref = block_of(self.kind, p, 1 - par, 0)
-                remote(ref, ref, fs.at[0, 0, 0], self.arrived(p, 1 - par, 0), to_y).wait_recv()
+            for m in range(self.plain):
+                for k in range(LINE):
+                    p = lax.rem(pos + k, LINE)
+                    ref = block_of(self.kind, p, 1 - par, m)
+                    remote(ref, ref, fs.at[0, 0, 0], self.arrived(p, 1 - par, m), to_y).wait_recv()
             for way in range(2):
                 for j in range(1, LINE):
                     p = pos - j if way == 0 else pos + j
                     last = (p >= 0) & (pos == LINE - 1) if way == 0 else (p < LINE) & (pos == 0)
-                    for m in range(1, micro):
+                    for m in range(self.plain, micro):
                         for q in (par, 1 - par):
                             ref = block_of(self.kind, p, q, m)
                             come = remote(ref, ref, fs.at[0, 0, 0], self.arrived(p, q, m), to_y)
                             pl.when(last)(come.wait_recv)
 
         def mixed_sent(self):
-            self.each(0, 0, 0, lambda c: c.wait_send())
-            for way in range(2):
-                for j in range(1, LINE):
-                    self.each(way, j, 0, lambda c: c.wait_send())
-            for m in range(1, micro):
+            for m in range(self.plain):
+                self.each(0, 0, m, lambda c: c.wait_send())
+                for way in range(2):
+                    for j in range(1, LINE):
+                        self.each(way, j, m, lambda c: c.wait_send())
+            for m in range(self.plain, micro):
                 self.wide_pair(m).wait_send()
                 for j in range(LINE):
                     for q in (par, 1 - par):
                         for way, (copy, when) in enumerate(self.wide(j, q, m)):
-                            if j == 0 and q is par:
-                                pl.when(when)(copy.wait_send)
-                                continue
                             pl.when(when)(copy.wait_send)
-                            if self.same or (j == 0 and way == 1):
+                            if self.same or j == 0 and (q is par or way == 1):
                                 continue
                             p = pos - j if way == 0 else pos + j
                             came = (p >= 0) if way == 0 else (p < LINE)
@@ -393,7 +384,7 @@
                 ref = block_of(self.kind, p, q, m)
                 remote(ref, ref, fs.at[0, 0, 0], self.arrived(p, q, m), to_y).wait_recv()
 
-    nm0, nm1, gd0, gd1 = Gather(0, 0), Gather(0, 1), Gather(1, 0), Gather(1, 1)
+    nm0, nm1, gd0, gd1 = Gather(0, 0, 1), Gather(0, 1, 1), Gather(1, 0, 1), Gather(1, 1, 1)
 
     def grad_rows(m):
         return pl.ds(pl.multiple_of(g * span + m * rows, rows), rows)
@@ -420,8 +411,7 @@
                 to = pl.ds(pl.multiple_of(g * span + m * rows + part * half, half), half)
                 gd_all[to] = (gin[pr].astype(F32) * live_of(m, part)).astype(BF)
             gd1.mixed_own(m)
-        for m in range(1, micro):
-            gd1.wide_on(0, m)
+        gd1.crossed()
         gd1.mixed_on(1)
 
     def x_swap(e, m):
@@ -518,7 +508,7 @@
 
         @pl.when(s == 1)
         def _():
-            nm1.own(m)
+            nm1.mixed_own(m)
 
         @pl.when((s == 0) & (m == 0))
         def _():
@@ -530,7 +520,7 @@
         gp[m] = slope.astype(BF)
         part = dot(h, wdown[...])
         give(1, m, part)
-        part_f[m] = r + part
+        rout[m] = r + part
 
     def act_copy(m):
         return local(act.at[m, pl.ds(0, half)], act_o.at[0, m], osem.at[m])
@@ -540,7 +530,7 @@
 
     def end_forward(m):
         x_swap(1, m).wait_recv()
-        act[m] = (part_f[m] + rbuf[1, m].astype(F32)).astype(BF)
+        act[m] = (rout[m] + rbuf[1, m].astype(F32)).astype(BF)
 
         @pl.when(s == 0)
         def _():
@@ -559,11 +549,9 @@
         gd1.mixed_on(2)
 
     each_micro(ffn_forward)
-    each_micro(end_forward)
-
-    @pl.when(s == 1)
-    def _():
-        gd1.mixed_on(3)
+    @pl.when(s == 0)
+    def _():
+        each_micro(end_forward)
 
 
     tile = hb.shape[0]
@@ -576,9 +564,8 @@
     def _():
         wupt[...] = wup[...].T
 
-        for m in range(1, micro):
-            nm0.wide_on(0, m)
-        for j in range(1, LINE):
+        nm0.crossed()
+        for j in range(1, LINE - 1):
             nm0.mixed_on(j)
 
     def ffn_back(m):
@@ -596,7 +583,8 @@
     def mixer_back(m):
         @pl.when((s == 1) & (m == 1))
         def _():
-            nm1.pass_both(1)
+            nm1.crossed()
+            nm1.mixed_on(1)
 
         x_swap(2, m).wait_recv()
         gn = part_f[m] + rbuf[2, m].astype(F32)
@@ -664,6 +652,15 @@
 
     each_micro(ffn_back)
 
+    @pl.when(s == 0)
+    def _():
+        nm0.mixed_on(LINE - 1)
+
+    @pl.when(s == 1)
+    def _():
+        each_micro(end_forward)
+        gd1.mixed_on(3)
+
     each_micro(mixer_back)
 
     late = y_copies(1)
@@ -695,45 +692,62 @@
     sb[1] = block.astype(BF)
 
     part_rows = hp.shape[0] // 2
-    chunk = part_rows // 4
+    most = part_rows // 4
+    cut_at = -(-most // 32) * 16
 
     class Line:
-        def __init__(self, n):
-            self.n = n
+        def __init__(self, whole):
+            self.whole = whole
+            ends = [most * (i + 1) for i in range(3 if whole else 1)]
+            self.ends = [0] + ends + [ends[-1] + cut_at, ends[-1] + most]
+            self.n = len(self.ends) - 1
+
+        def size(self, j):
+            return self.ends[j + 1] - self.ends[j]
+
+        def at(self, near, j):
+            group = side if near else 1 - side
+            return group * self.ends[-1] + self.ends[j]
 
         def piece(self, near, j):
-            group = side if near else 1 - side
-            return pl.ds(pl.multiple_of((group * self.n + j) * chunk, 16), chunk)
+            return pl.ds(pl.multiple_of(self.at(near, j), 16), self.size(j))
 
         def final(self, near, j):
-            if self.n == 4:
-                return fin.at[self.piece(near, j)]
-            group = side if near else 1 - side
-            return fin.at[pl.ds(pl.multiple_of(par * part_rows + (group * self.n + j) * chunk, 16), chunk)]
+            first_row = self.at(near, j) + (0 if self.whole else par * part_rows)
+            return fin.at[pl.ds(pl.multiple_of(first_row, 16), self.size(j))]
+
+        def come_out(self, near, j):
+            return from_out.at[5 * near + j, pl.ds(0, self.size(j))]
+
+        def come_opp(self, j):
+            return from_opp.at[j, pl.ds(0, self.size(j))]
+
+        def come_pair(self, j):
+            return from_pair.at[j, pl.ds(0, self.size(j))]
 
         def send_in(self, near, j):
-            i = 4 * near + j
-            return remote(hp.at[self.piece(near, j)], from_out.at[i], ars.at[i], arr.at[i], to_mate)
+            i = 5 * near + j
+            return remote(hp.at[self.piece(near, j)], self.come_out(near, j), ars.at[i], arr.at[i], to_mate)
 
         def send_over(self, j):
-            return remote(hp.at[self.piece(0, j)], from_opp.at[j], ars.at[j], arr.at[8 + j], to_opp)
+            return remote(hp.at[self.piece(0, j)], self.come_opp(j), ars.at[j], arr.at[10 + j], to_opp)
 
         def total_over(self, j):
             ref = self.final(1, j)
-            return remote(ref, ref, ars.at[4 + j], arr.at[12 + j], to_opp)
+            return remote(ref, ref, ars.at[5 + j], arr.at[15 + j], to_opp)
 
         def total_out(self, near, j):
-            i = 4 * near + j
+            i = 5 * near + j
             ref = self.final(near, j)
-            return remote(ref, ref, ars.at[8 + i], arr.at[i], to_mate)
+            return remote(ref, ref, ars.at[10 + i], arr.at[i], to_mate)
 
         def total_pair(self, near, j):
-            i = 16 + 2 * near + j if self.n == 2 else 8 + 4 * near + j
+            i = 20 + 3 * near + j
             ref = self.final(near, j)
             return remote(ref, ref, ars.at[i], arr.at[i], to_y)
 
         def trade(self, j):
-            return remote(hp.at[self.piece(1, j)], from_pair.at[j], ars.at[16 + j], arr.at[16 + j], to_y)
+            return remote(hp.at[self.piece(1, j)], self.come_pair(j), ars.at[20 + j], arr.at[20 + j], to_y)
 
         def start(self, lo, hi):
             @pl.when(outer)
@@ -747,7 +761,7 @@
             def _():
                 self.send_in(0, j).wait_recv()
                 p = self.piece(0, j)
-                hp[p] = (hp[p].astype(F32) + from_out[j].astype(F32)).astype(BF)
+                hp[p] = (hp[p].astype(F32) + self.come_out(0, j)[...].astype(F32)).astype(BF)
                 self.send_over(j).start()
 
         def total(self, j):
@@ -756,8 +770,8 @@
                 self.send_in(1, j).wait_recv()
                 self.send_over(j).wait_recv()
                 p = self.piece(1, j)
-                tot = hp[p].astype(F32) + from_out[4 + j].astype(F32) + from_opp[j].astype(F32)
-                if self.n == 4:
+                tot = hp[p].astype(F32) + self.come_out(1, j)[...].astype(F32) + self.come_opp(j)[...].astype(F32)
+                if self.whole:
                     hp[p] = tot.astype(BF)
                     self.trade(j).start()
                 else:
@@ -765,7 +779,7 @@
                     self.total_out(1, j).start()
                     self.total_over(j).start()
 
-            if self.n == 2:
+            if not self.whole:
                 @pl.when(outer)
                 def _():
                     self.total_out(1, j).wait_recv()
@@ -776,7 +790,7 @@
             @pl.when(inner)
             def _():
                 self.trade(j).wait_recv()
-                tot = hp[self.piece(1, j)].astype(F32) + from_pair[j].astype(F32)
+                tot = hp[self.piece(1, j)].astype(F32) + self.come_pair(j)[...].astype(F32)
                 self.final(1, j)[...] = tot.astype(BF)
                 self.total_out(1, j).start()
                 self.total_over(j).start()
@@ -794,7 +808,7 @@
                 self.total_over(j).wait_recv()
                 self.total_out(0, j).start()
 
-            if self.n == 2:
+            if not self.whole:
                 @pl.when(outer)
                 def _():
                     self.total_out(0, j).wait_recv()
@@ -804,11 +818,9 @@
                 self.across(0, j)
 
         def last(self):
-            if self.n == 2:
-                for near in range(2):
-                    for j in range(2):
-                        self.total_pair(near, j).wait_recv()
-                return
+            for near in range(2):
+                for j in range(self.n):
+                    self.total_pair(near, j).wait_recv()
 
         def finish(self):
             for j in range(self.n):
@@ -821,16 +833,16 @@
                 def _():
                     self.send_over(j).wait_send()
                     self.total_over(j).wait_send()
-                    if self.n == 4:
+                    if self.whole:
                         self.trade(j).wait_send()
 
                 mine = par == j % 2
                 for near in range(2):
                     pl.when(inner)(self.total_out(near, j).wait_send)
-                    if self.n == 2:
+                    if not self.whole:
                         self.total_pair(near, j).wait_send()
 
-    first, second = Line(2), Line(4)
+    first, second = Line(False), Line(True)
 
     @pl.when(s == 0)
     def _():
@@ -849,7 +861,7 @@
         hp[v_rows] = v_tot.astype(BF)
         hp[m_rows] = (dot(mtb[...], gbr[:, m_part]) + dot(ymtb[...], ygbr[...])).astype(BF)
         hp[s_rows] = (sb[par].astype(F32) + ysb[...].astype(F32)).astype(BF)
-        first.start(0, 2)
+        first.start(0, first.n)
 
     @pl.when(s == 1)
     def _():
@@ -863,13 +875,12 @@
             hp[pl.ds(3 * width + c * hw, hw)] = tot[:, c * hw : (c + 1) * hw]
         for e in range(2):
             hp[pl.ds(3 * width + cut * hw + e * hs, hs)] = sb[e]
-        for m in range(1, micro):
-            gd0.wide_on(0, m)
+        gd0.crossed()
         second.start(0, 2)
         gd0.mixed_on(1)
-        nm1.pass_both(2)
+        nm1.mixed_on(2)
         gd0.mixed_on(2)
-        nm1.pass_both(3)
+        nm1.mixed_on(3)
         gd1.mixed_take()
 
     @pl.when(s == 0)
@@ -883,8 +894,8 @@
     def _():
         second.collect(0)
         gd0.mixed_on(3)
-        for k in range(1, GROUP, 2):
-            nm1.take(lax.rem(g + k, GROUP))
+        second.start(2, second.n)
+        nm1.mixed_take()
 
     def up_copy(t):
         return local(wup.at[:, hid_rows(t)], up_o.at[:, hid_rows(t)], tsem.at[0, t])
@@ -914,29 +925,36 @@
         (0, True): {
             0: [("total", 0)],
             1: [("collect", 1)],
-            2: [("passed", 0), ("total", 1)],
-            3: [("passed", 1)],
+            2: [("collect", 2), ("passed", 0), ("total", 1)],
+            3: [("total", 2), ("passed", 1)],
+            4: [("passed", 2)],
         },
-        (0, False): {2: [("total", 0)], 3: [("passed", 0), ("total", 1)], 4: [("passed", 1)]},
+        (0, False): {
+            2: [("total", 0)],
+            3: [("passed", 0), ("total", 1)],
+            4: [("total", 2), ("passed", 1)],
+            5: [("passed", 2)],
+        },
         (1, True): {
             0: [("total", 0), ("collect", 1)],
             1: [("total", 1)],
             2: [("settle", 0)],
-            3: [("settle", 1), ("collect", 2)],
-            4: [("passed", 0), ("total", 2), ("collect", 3)],
+            3: [("collect", 2), ("settle", 1)],
+            4: [("collect", 3), ("passed", 0), ("total", 2)],
             5: [
+                ("collect", 4),
                 ("passed", 1),
+                ("total", 3),
                 ("settle", 2),
-                ("total", 3),
+                ("total", 4),
+                ("settle", 3),
                 ("passed", 2),
-                ("settle", 3),
+                ("settle", 4),
                 ("passed", 3),
+                ("passed", 4),
             ],
         },
-        (1, False): {
-            0: [("start", 2, 4)],
-            5: [(f, j) for j in range(4) for f in ("settle", "passed")],
-        },
+        (1, False): {5: [(f, j) for j in range(5) for f in ("settle", "passed")]},
     }
 
     def one_tile(t, carry):
@@ -955,10 +973,6 @@
     @pl.when(s == 0)
     def _():
         first.last()
-
-    @pl.when(s == 1)
-    def _():
-        second.last()
 
     def outs_of(layer, out_copy):
         if layer == 1:
@@ -1025,7 +1039,7 @@
     def _():
         gd1.mixed_sent()
         gd0.mixed_sent()
-        nm1.sent()
+        nm1.mixed_sent()
 
     @pl.when(s == 0)
     def _():
@@ -1148,6 +1162,7 @@
             vm((256, GROUP * span), b),
             vm((micro, rows, ff), b),
             vm((micro, rows, width), f),
+            vm((micro, rows, width), f),
             vm((micro, rows, width), b),
             vm((span, width), b),
             vm((span, width), b),
@@ -1164,11 +1179,11 @@
             vm((hs, hw), b),
             vm((2 * part_rows, hw), b),
             vm((2 * part_rows, hw), b),
-            vm((8, part_rows // 4, hw), b),
-            vm((4, part_rows // 4, hw), b),
-            vm((4, part_rows // 4, hw), b),
+            vm((10, part_rows // 4, hw), b),
+            vm((5, part_rows // 4, hw), b),
+            vm((5, part_rows // 4, hw), b),
             vm((LINE, span, width), b),
-            vm((micro - 1, 2, LINE, rows, width), b),
+            vm((micro, 2, LINE, rows, width), b),
             dma((4 + micro,)),
             dma((5 * micro,)),
             dma((5 * micro,)),
@@ -1177,11 +1192,11 @@
             dma((2, micro, GROUP)),
             dma((micro, LINE)),
             dma((3, micro, 20)),
-            dma((micro - 1, GROUP)),
+            dma((micro, GROUP)),
             dma((3 + 3 * micro,)),
             dma((3 + 3 * micro,)),
-            dma((20,)),
-            dma((20,)),
+            dma((26,)),
+            dma((26,)),
             dma((2 * micro + 10,)),
             dma((2, ff // 256)),
         ],

time: 148 us -> 141 us (0.953)
  Pallas kernels: 147 us -> 140 us
    pallas_call x1, Pallas kernels: 139 us -> 133 us  [on_device(): pl.pallas_call(kernel, out_shape=[out((1, micro, half, width)), out((1, m...]
where the time goes in v4:
time: 141 us
  Pallas kernels  140 us (99%)
    pallas_call x1, Pallas kernels, on_device(): pl.pallas_call(kernel, out_shape=[out((1, micro, half, width)), out((1, m...  133 us
    pallas_call x1, Pallas kernels, on_device(): pl.pallas_call(widen, out_shape=[out(act.shape), out(ig.shape)] + [out(o,...  7.5 us

profile of v4, /device:TPU:1, one launch (start us, length us, event | category | flops | bytes accessed | tf_op | source)
XLA Modules:
  0.0 141.1 jit_solution(10509353712609446376)
XLA Ops:
  0.6 132.8 %shard_map.178 = (bf16[1,2,64,768]{3,2,1,0:T(8,128)(2,1)}, bf16[1,2,64,768]{3,2,1,0:T(8,128)(2,1)}, bf16[2304,384]{1,0:T(8,128)(2,1)}, bf16[384,768]{1,0:T(8,128...) custom-call(bf16[2,64,768]{2,1,0:T(8,128)(2,1)} %x_in.1, ...), custom_call_target="tpu_custom_call" | custom-call | tf_op jit(solution)/shard_map/pallas_call | solution.py:1126
  133.4 7.5 %shard_map.179 = (bf16[1,2,64,768]{3,2,1,0:T(8,128)(2,1)}, bf16[1,2,64,768]{3,2,1,0:T(8,128)(2,1)}, f32[1,3,768,384]{3,2,1,0:T(8,128)}, f32[1,384,768]{2,1,0:T(8...) custom-call(bf16[1,2,64,768]{3,2,1,0:T(8,128)(2,1)} %get-tuple-eleme, ...), custom_call_target="tpu_custom_call" | custom-call | tf_op jit(solution)/shard_map/pallas_call | solution.py:1217

commit v5 on v4

--- a/solution.py
+++ b/solution.py
@@ -213,7 +213,7 @@
             return self.arrived(p, par, m) if self.same else ha.at[m, p]
 
         def sending(self, i, m):
-            return fs.at[self.kind if self.same else 2, m, i]
+            return fs.at[self.kind if self.same else 2, i + 12 * m]
 
         def to(self, core, p, q):
             return (core, base + p * 2 + q, xi)
@@ -315,7 +315,7 @@
                     continue
                 if j == 0:
                     ref = self.wide_held(pos, q, m)
-                    remote(ref, ref, fs.at[0, 0, 0], self.wide_arrived(pos, q, m), to_y).wait_recv()
+                    remote(ref, ref, fs.at[0, 0], self.wide_arrived(pos, q, m), to_y).wait_recv()
                     if not self.same:
                         self.wide_home(0, 0, q, m).start()
                 for way, (copy, when) in enumerate(self.wide(j, q, m)):
@@ -349,7 +349,7 @@
                 for k in range(LINE):
                     p = lax.rem(pos + k, LINE)
                     ref = block_of(self.kind, p, 1 - par, m)
-                    remote(ref, ref, fs.at[0, 0, 0], self.arrived(p, 1 - par, m), to_y).wait_recv()
+                    remote(ref, ref, fs.at[0, 0], self.arrived(p, 1 - par, m), to_y).wait_recv()
             for way in range(2):
                 for j in range(1, LINE):
                     p = pos - j if way == 0 else pos + j
@@ -357,7 +357,7 @@
                     for m in range(self.plain, micro):
                         for q in (par, 1 - par):
                             ref = block_of(self.kind, p, q, m)
-                            come = remote(ref, ref, fs.at[0, 0, 0], self.arrived(p, q, m), to_y)
+                            come = remote(ref, ref, fs.at[0, 0], self.arrived(p, q, m), to_y)
                             pl.when(last)(come.wait_recv)
 
         def mixed_sent(self):
@@ -382,7 +382,7 @@
             p, q = lax.div(i, 2), lax.rem(i, 2)
             for m in range(micro):
                 ref = block_of(self.kind, p, q, m)
-                remote(ref, ref, fs.at[0, 0, 0], self.arrived(p, q, m), to_y).wait_recv()
+                remote(ref, ref, fs.at[0, 0], self.arrived(p, q, m), to_y).wait_recv()
 
     nm0, nm1, gd0, gd1 = Gather(0, 0, 1), Gather(0, 1, 1), Gather(1, 0, 1), Gather(1, 1, 1)
 
@@ -584,7 +584,6 @@
         @pl.when((s == 1) & (m == 1))
         def _():
             nm1.crossed()
-            nm1.mixed_on(1)
 
         x_swap(2, m).wait_recv()
         gn = part_f[m] + rbuf[2, m].astype(F32)
@@ -692,14 +691,20 @@
     sb[1] = block.astype(BF)
 
     part_rows = hp.shape[0] // 2
-    most = part_rows // 4
-    cut_at = -(-most // 32) * 16
+    most = 464
+
+    def ends_of(total, shares):
+        out = [0]
+        for share in shares:
+            out.append(min(total, -(-total * share // 1600) * 16))
+        return out
+
+    WHOLE, HALF = (25, 50, 75, 88, 100), (50, 76, 100)
 
     class Line:
         def __init__(self, whole):
             self.whole = whole
-            ends = [most * (i + 1) for i in range(3 if whole else 1)]
-            self.ends = [0] + ends + [ends[-1] + cut_at, ends[-1] + most]
+            self.ends = ends_of(part_rows * (2 if whole else 1) // 2, WHOLE if whole else HALF)
             self.n = len(self.ends) - 1
 
         def size(self, j):
@@ -876,6 +881,7 @@
         for e in range(2):
             hp[pl.ds(3 * width + cut * hw + e * hs, hs)] = sb[e]
         gd0.crossed()
+        nm1.mixed_on(1)
         second.start(0, 2)
         gd0.mixed_on(1)
         nm1.mixed_on(2)
@@ -1179,9 +1185,9 @@
             vm((hs, hw), b),
             vm((2 * part_rows, hw), b),
             vm((2 * part_rows, hw), b),
-            vm((10, part_rows // 4, hw), b),
-            vm((5, part_rows // 4, hw), b),
-            vm((5, part_rows // 4, hw), b),
+            vm((10, 464, hw), b),
+            vm((5, 464, hw), b),
+            vm((5, 464, hw), b),
             vm((LINE, span, width), b),
             vm((micro, 2, LINE, rows, width), b),
             dma((4 + micro,)),
@@ -1191,7 +1197,7 @@
             dma((2 * micro,)),
             dma((2, micro, GROUP)),
             dma((micro, LINE)),
-            dma((3, micro, 20)),
+            dma((3, 12 * (micro - 1) + 20)),
             dma((micro, GROUP)),
             dma((3 + 3 * micro,)),
             dma((3 + 3 * micro,)),

time: 141 us -> 141 us (level)
  no operation moved by 1% of the time
where the time goes in v5:
time: 141 us; the launch traced here: 140 us
  Pallas kernels  140 us (99%)
    pallas_call x1, Pallas kernels, on_device(): pl.pallas_call(kernel, out_shape=[out((1, micro, half, width)), out((1, m...  132 us
    pallas_call x1, Pallas kernels, on_device(): pl.pallas_call(widen, out_shape=[out(act.shape), out(ig.shape)] + [out(o,...  7.5 us

profile of v5, /device:TPU:1, one launch (start us, length us, event | category | flops | bytes accessed | tf_op | source)
XLA Modules:
  0.0 140.4 jit_solution(13682001314825388977)
XLA Ops:
  0.6 132.0 %shard_map.178 = (bf16[1,2,64,768]{3,2,1,0:T(8,128)(2,1)}, bf16[1,2,64,768]{3,2,1,0:T(8,128)(2,1)}, bf16[2304,384]{1,0:T(8,128)(2,1)}, bf16[384,768]{1,0:T(8,128...) custom-call(bf16[2,64,768]{2,1,0:T(8,128)(2,1)} %x_in.1, ...), custom_call_target="tpu_custom_call" | custom-call | tf_op jit(solution)/shard_map/pallas_call | solution.py:1132
  132.7 7.5 %shard_map.179 = (bf16[1,2,64,768]{3,2,1,0:T(8,128)(2,1)}, bf16[1,2,64,768]{3,2,1,0:T(8,128)(2,1)}, f32[1,3,768,384]{3,2,1,0:T(8,128)}, f32[1,384,768]{2,1,0:T(8...) custom-call(bf16[1,2,64,768]{3,2,1,0:T(8,128)(2,1)} %get-tuple-eleme, ...), custom_call_target="tpu_custom_call" | custom-call | tf_op jit(solution)/shard_map/pallas_call | solution.py:1223

commit v6 on v5

--- a/solution.py
+++ b/solution.py
@@ -822,6 +822,17 @@
             else:
                 self.across(0, j)
 
+        def ready(self):
+            rows_done = [(0, self.ends[3]), (self.ends[-1], min(self.ends[-1] + self.ends[3], 3 * width))]
+            return [
+                local(fin.at[pl.ds(lo, hi - lo)], qkv_o.at[pl.ds(lo, hi - lo)], osem.at[2 * micro + 8 + i])
+                for i, (lo, hi) in enumerate(rows_done)
+            ]
+
+        def early(self):
+            for c in self.ready():
+                c.start()
+
         def last(self):
             for near in range(2):
                 for j in range(self.n):
@@ -955,12 +966,17 @@
                 ("total", 4),
                 ("settle", 3),
                 ("passed", 2),
+                ("early",),
                 ("settle", 4),
                 ("passed", 3),
                 ("passed", 4),
             ],
         },
-        (1, False): {5: [(f, j) for j in range(5) for f in ("settle", "passed")]},
+        (1, False): {
+            5: [(f, j) for j in range(3) for f in ("settle", "passed")]
+            + [("early",)]
+            + [(f, j) for j in range(3, 5) for f in ("settle", "passed")]
+        },
     }
 
     def one_tile(t, carry):
@@ -982,7 +998,8 @@
 
     def outs_of(layer, out_copy):
         if layer == 1:
-            out_copy(fin.at[pl.ds(0, 3 * width)], qkv_o)
+            lo, hi = second.ends[3], second.ends[-1]
+            out_copy(fin.at[pl.ds(lo, hi - lo)], qkv_o.at[pl.ds(lo, hi - lo)])
             for c in range(cut):
                 out_copy(fin.at[pl.ds(3 * width + c * hw, hw)], mix_o.at[:, pl.ds(c * hw, hw)])
             for e in range(2):
@@ -1021,6 +1038,8 @@
     @pl.when(s == 1)
     def _():
         ended(1)
+        for c in second.ready():
+            c.wait()
 
     @pl.when(s == 0)
     def _():

time: 141 us -> 140 us (level)
  no operation moved by 1% of the time
where the time goes in v6:
time: 140 us
  Pallas kernels  139 us (99%)
    pallas_call x1, Pallas kernels, on_device(): pl.pallas_call(kernel, out_shape=[out((1, micro, half, width)), out((1, m...  132 us
    pallas_call x1, Pallas kernels, on_device(): pl.pallas_call(widen, out_shape=[out(act.shape), out(ig.shape)] + [out(o,...  7.5 us

profile of v6, /device:TPU:1, one launch (start us, length us, event | category | flops | bytes accessed | tf_op | source)
XLA Modules:
  0.0 139.9 jit_solution(9769684127287866106)
XLA Ops:
  0.6 131.5 %shard_map.178 = (bf16[1,2,64,768]{3,2,1,0:T(8,128)(2,1)}, bf16[1,2,64,768]{3,2,1,0:T(8,128)(2,1)}, bf16[2304,384]{1,0:T(8,128)(2,1)}, bf16[384,768]{1,0:T(8,128...) custom-call(bf16[2,64,768]{2,1,0:T(8,128)(2,1)} %x_in.1, ...), custom_call_target="tpu_custom_call" | custom-call | tf_op jit(solution)/shard_map/pallas_call | solution.py:1151
  132.2 7.5 %shard_map.179 = (bf16[1,2,64,768]{3,2,1,0:T(8,128)(2,1)}, bf16[1,2,64,768]{3,2,1,0:T(8,128)(2,1)}, f32[1,3,768,384]{3,2,1,0:T(8,128)}, f32[1,384,768]{2,1,0:T(8...) custom-call(bf16[1,2,64,768]{3,2,1,0:T(8,128)(2,1)} %get-tuple-eleme, ...), custom_call_target="tpu_custom_call" | custom-call | tf_op jit(solution)/shard_map/pallas_call | solution.py:1242
